TPU v7x, 32 devices: a whole 2x2x4 slice. The times are simulated.
32 devices in a mesh: lon: 4 (over y, x), lat: 8 (over z, core).
Axes of the slice: x: 2, y: 2, z: 4, core: 2. Of those that a mesh axis runs over, the one named last changes fastest.
Arguments:
- adjoint_in: float32 [5, 192, 192, 128], P(None, 'lon', 'lat'), may hold values from -6 to 6
- departures: float32 [4, 8, 1024, 128], P('lon', 'lat'), may hold values from -6 to 6
- obs_band: int32 [4, 8, 1024, 1], P('lon', 'lat'), may hold values from 0 to 7; in each aligned block of 1024 rows (0 to 1023, 1024 to 2047, ..., all dimensions but the last counted through in order) at most 384 rows name the same one
- obs_station: int32 [4, 8, 1024], P('lon', 'lat'), may hold values from 0 to 511
- obs_var: int32 [4, 8, 1024], P('lon', 'lat'), may hold values from 0 to 4
- counts: int32 [4, 8], P('lon', 'lat'), may hold values from 512 to 1024, as said below
- station_cell: int32 [4, 8, 512], P('lon', 'lat'), may hold values from 0 to 1151
- coefficients: float32 [3, 192, 192, 128], P(None, 'lon', 'lat'), as said below
Outputs:
- adjoint_out: float32 [5, 192, 192, 128], P(None, 'lon', 'lat')
Inputs may be any that keep to these rules, and one draw needn't show every extreme that they name: `obs_band`: among the 1024 blocks of one device at most 384 name the same band, and on some device exactly 384 do. `counts`: some device has exactly 1024 live blocks. `coefficients`: the diffusivity lies between 0.03 and 0.12.
All inputs are finite; a program needn't handle non-finite values.
Results may differ from a plain program's by a relative error of at most 0.00013.
Values sent between devices are 32-bit elements; how exact they have to be, the bound alone decides.
No kernel may reach another device: no remote copies, remote signals or barrier semaphores. Data moves between devices by JAX's collectives and lax.ppermute only.
A program may use at most 384 MiB of HBM per device.

v0:
```python
import jax
import jax.numpy as jnp
from jax import lax
from jax.sharding import PartitionSpec as P

STATIONS = 512


ADVECT_SCALE = 0.2


def padded_2(block, sides, width, periodic):
    for axis, dim in sides:
        count = lax.axis_size(axis)
        forward = [(i, i + 1) for i in range(count - 1)]
        if periodic:
            forward.append((count - 1, 0))
        backward = [(target, source) for source, target in forward]
        low = lax.ppermute(
            lax.slice_in_dim(block, block.shape[dim] - width, None, axis=dim), axis, forward
        )
        high = lax.ppermute(lax.slice_in_dim(block, 0, width, axis=dim), axis, backward)
        block = jnp.concatenate([low, block, high], axis=dim)
    return block


def advance(padded, coeffs):
    centre = padded[:, 1:-1, 1:-1]
    east_side = padded[:, 2:, 1:-1]
    west_side = padded[:, :-2, 1:-1]
    north_side = padded[:, 1:-1, 2:]
    south_side = padded[:, 1:-1, :-2]
    wind_east = coeffs[0, 1:-1, 1:-1]
    wind_west = coeffs[0, :-2, 1:-1]
    wind_north = coeffs[1, 1:-1, 1:-1]
    wind_south = coeffs[1, 1:-1, :-2]
    kappa_all = coeffs[2]
    kappa_centre = kappa_all[1:-1, 1:-1]
    kappa_east = 0.5 * (kappa_centre + kappa_all[2:, 1:-1])
    kappa_west = 0.5 * (kappa_centre + kappa_all[:-2, 1:-1])
    kappa_north = 0.5 * (kappa_centre + kappa_all[1:-1, 2:])
    kappa_south = 0.5 * (kappa_centre + kappa_all[1:-1, :-2])
    level_zero = jnp.zeros_like(kappa_centre[..., :1])
    kappa_up = jnp.concatenate(
        [0.5 * (kappa_centre[..., :-1] + kappa_centre[..., 1:]), level_zero], -1
    )
    kappa_down = jnp.concatenate([level_zero, kappa_up[..., :-1]], -1)
    centre_zero = jnp.zeros_like(centre[..., :1])
    above = jnp.concatenate([centre[..., 1:], centre_zero], -1)
    below = jnp.concatenate([centre_zero, centre[..., :-1]], -1)
    transport = wind_east * (east_side - centre) + wind_west * (centre - west_side)
    transport = transport + wind_north * (north_side - centre) + wind_south * (centre - south_side)
    mixing = kappa_east * (east_side - centre) - kappa_west * (centre - west_side)
    mixing = mixing + kappa_north * (north_side - centre) - kappa_south * (centre - south_side)
    mixing = mixing + kappa_up * (above - centre) - kappa_down * (centre - below)
    return centre + ADVECT_SCALE * transport + mixing


def extend(values, depth):
    widened = padded_2(values, (("lon", 1),), depth, True)
    return padded_2(widened, (("lat", 2),), depth, False)


def station_sums(amounts, codes, weight, pair_count):
    selector = (codes[None, :] == jnp.arange(pair_count, dtype=jnp.int32)[:, None]).astype(
        jnp.float32
    )
    selector = selector * weight[None, :]
    return jnp.dot(
        selector, amounts, precision=lax.Precision.HIGHEST, preferred_element_type=jnp.float32
    )


def body(
    adjoint_in, departures, obs_band, obs_station, obs_var, counts, station_cell, coefficients
):
    var_count, lon_cells, lat_cells, level_count = adjoint_in.shape
    cells = lon_cells * lat_cells
    slots = departures.shape[2]
    pair_count = var_count * STATIONS
    table = station_cell[0, 0]
    live = (jnp.arange(slots, dtype=jnp.int32) < counts[0, 0]).astype(jnp.float32)
    amounts = departures[0, 0] * live[:, None]
    codes = obs_var[0, 0] * STATIONS + obs_station[0, 0]
    bands = obs_band[0, 0, :, 0]
    my_band = lax.axis_index("lat")
    piece_amounts = lax.all_gather(amounts, "lat", axis=0, tiled=True)
    piece_codes = lax.all_gather(codes, "lat", axis=0, tiled=True)
    piece_bands = lax.all_gather(bands, "lat", axis=0, tiled=True)
    keep = (piece_bands == my_band).astype(jnp.float32)
    sums = station_sums(piece_amounts, piece_codes, keep, pair_count)
    cell_map = (table[None, :] == jnp.arange(cells, dtype=jnp.int32)[:, None]).astype(jnp.float32)
    added = jnp.einsum(
        "cs,vsl->vcl",
        cell_map,
        sums.reshape(var_count, STATIONS, level_count),
        precision=lax.Precision.HIGHEST,
        preferred_element_type=jnp.float32,
    )
    forced = adjoint_in + added.reshape(adjoint_in.shape)
    near_coeffs = extend(coefficients, 1)
    first = advance(extend(forced, 1), near_coeffs)
    result = advance(extend(first, 1), near_coeffs)
    return result


def solution(mesh):
    in_specs = (
        P(None, "lon", "lat", None),
        P("lon", "lat", None, None),
        P("lon", "lat", None, None),
        P("lon", "lat", None),
        P("lon", "lat", None),
        P("lon", "lat"),
        P("lon", "lat", None),
        P(None, "lon", "lat", None),
    )
    out_specs = P(None, "lon", "lat", None)
    return jax.shard_map(body, mesh=mesh, in_specs=in_specs, out_specs=out_specs, check_vma=False)
```

profile of v0, /device:TPU:1, one launch (start us, length us, event | category | flops | bytes accessed | tf_op | source)
XLA Modules:
  0.0 192.6 jit_solution(16547333974693041643)
XLA Ops:
  7.3 2.0 %bitcast_multiply_fusion = f32[1024,128]{1,0:T(8,128)} fusion(f32[1,1,1024,128]{3,2,1,0:T(8,128)} %param.9, f32[1024]{0:T(1024)S(1)} %fusion.24), kind=kLoop, calls=%fused_computation.59 | loop fusion | flops 131072 | bytes 1052672 | tf_op jit(solution)/shard_map/mul | solution.py:83
  9.4 1.4 fusion.30
  10.8 3.0 %collective-permute-start.4 = (f32[3,1,24,128]{3,1,2,0:T(1,128)}, f32[3,1,24,128]{3,1,2,0:T(1,128)}, u32[]{:S(2)}, u32[]{:S(2)}) collective-permute-start(f32[3,1,24,128]{3,1,2,0:T(1,128)} %bitcast.14), channel_id=1, source_target_pairs={{8,0},{16,8},{24,16},{0,24},{9,1},{17,9},{25,17},{1,25},{10,2},{18... | collective-permute-start | bytes 110600 | tf_op jit(solution)/shard_map/ppermute | solution.py:22
  13.8 15.3 %all-gather.1 = s32[1,1,8192,1]{2,3,1,0:T(1,128)S(1)} all-gather(s32[1,1,1024,1]{2,3,1,0:T(1,128)} %param.10), channel_id=3, replica_groups=mesh['lon'=4,'lat'=8] {'lat'}, dimensions={2}, use_global_device_ids=true | all-gather | bytes 36864 | tf_op jit(solution)/shard_map/all_gather | solution.py:89
  30.8 15.0 %all-gather = s32[1,1,8192]{2,1,0:T(1,128)} all-gather(s32[1,1,1024]{2,1,0:T(1,128)S(1)} %multiply_add_fusion), channel_id=2, replica_groups=mesh['lon'=4,'lat'=8] {'lat'}, dimensions={2}, use_global_device_ids=true | all-gather | bytes 36864 | tf_op jit(solution)/shard_map/all_gather | solution.py:88
  46.5 3.2 %collective-permute-start.5 = (f32[3,50,1,128]{3,1,2,0:T(8,128)S(1)}, f32[3,50,1,128]{3,1,2,0:T(8,128)S(1)}, u32[]{:S(2)}, u32[]{:S(2)}) collective-permute-start(f32[3,50,1,128]{3,1,2,0:T(8,128)S(1)} %get-tuple-element.17), channel_id=1, source_target_pairs={{0,1},{1,2},{2,3},{3,4},{4,5},{5,6},{6,7},{8,9},{9,10},{10,11},{11... | collective-permute-start | bytes 230408 | tf_op jit(solution)/shard_map/ppermute | solution.py:19
  49.8 1.9 collective-permute-start.7
  51.7 2.0 %slice_bitcast_fusion.1 = (f32[48,24,128]{2,1,0:T(8,128)}, f32[48,24,128]{2,1,0:T(8,128)}, f32[48,24,128]{2,1,0:T(8,128)}) fusion(f32[3,48,24,128]{3,2,1,0:T(8,128)S(1)} %copy-done, f32[3,1,24,128]{3,2,1,0:T(8,128)} %bitcast.11), kind=kLoop, calls=%fused_computation.58 | loop fusion | flops 147456 | bytes 4755456 | tf_op jit(solution)/shard_map/mul | solution.py:51
  53.7 2.8 %collective-permute-done.7 = f32[3,50,1,128]{3,1,2,0:T(8,128)S(1)} collective-permute-done((f32[3,50,1,128]{3,1,2,0:T(8,128)S(1)}, f32[3,50,1,128]{3,1,2,0:T(8,128)S(1)}, u32[]{:S(2)}, u32[]{:S(2)}) %collective-permute-start.7) | collective-permute-done | bytes 76832 | tf_op jit(solution)/shard_map/ppermute | solution.py:22
  56.5 0.8 fusion.16
  58.0 1.6 fusion.21
  59.5 0.9 all-gather.4.cloned.1.call-done
  60.4 70.4 %fusion = f32[2560,128]{1,0:T(8,128)S(1)} fusion(f32[8192,128]{1,0:T(8,128)} %all-gather.4.cloned.1.call-done, f32[8192]{0:T(1024)S(1)} %bitcast.33, s32[8192]{0:T(1024)S(1)} %bitcast.32), kind=kOutput, calls=%fused_computation | convolution fusion | flops 32254197760 | bytes 5570560 | tf_op jit(solution)/shard_map/dot_general | solution.py:69
  130.9 7.0 %convolution_bitcast_fusion = f32[5,1152,128]{1,2,0:T(8,128)} fusion(f32[5,512,128]{2,1,0:T(8,128)S(1)} %bitcast.31, s32[512]{0:T(512)S(1)} %bitcast.34), kind=kOutput, calls=%fused_computation.6 | convolution fusion | flops 4530438144 | bytes 4261888 | tf_op jit(solution)/shard_map/cs,vsl->vcl/dot_general | solution.py:93
  137.9 4.8 %copy.14 = f32[5,1152,128]{2,1,0:T(8,128)} copy(f32[5,1152,128]{1,2,0:T(8,128)} %convolution_bitcast_fusion) | data formatting | bytes 5898240 | tf_op jit(solution)/shard_map/cs,vsl->vcl/transpose | solution.py:93
  142.7 3.0 %add.85 = f32[5,48,24,128]{3,2,1,0:T(8,128)S(1)} add(f32[5,48,24,128]{3,2,1,0:T(8,128)} %param.8, f32[5,48,24,128]{3,2,1,0:T(8,128)} %bitcast.30) | non-fusion elementwise | flops 737280 | bytes 8847360 | tf_op jit(solution)/shard_map/add | solution.py:100
  145.8 1.2 collective-permute-start.2
  147.0 1.2 collective-permute-start
  150.2 0.9 collective-permute-done
  151.3 3.2 %collective-permute-start.3 = (f32[5,50,1,128]{3,2,1,0:T(1,128)S(1)}, f32[5,50,1,128]{3,2,1,0:T(1,128)S(1)}, u32[]{:S(2)}, u32[]{:S(2)}) collective-permute-start(f32[5,50,1,128]{3,2,1,0:T(1,128)S(1)} %get-tuple-element.7), channel_id=1, source_target_pairs={{1,0},{2,1},{3,2},{4,3},{5,4},{6,5},{7,6},{9,8},{10,9},{11,10},{12... | collective-permute-start | bytes 384008 | tf_op jit(solution)/shard_map/ppermute | solution.py:22
  154.6 2.5 %collective-permute-start.6 = (f32[5,50,1,128]{3,2,1,0:T(1,128)S(1)}, f32[5,50,1,128]{3,2,1,0:T(1,128)S(1)}, u32[]{:S(2)}, u32[]{:S(2)}) collective-permute-start(f32[5,50,1,128]{3,2,1,0:T(1,128)S(1)} %get-tuple-element.8), channel_id=1, source_target_pairs={{0,1},{1,2},{2,3},{3,4},{4,5},{5,6},{6,7},{8,9},{9,10},{10,11},{11... | collective-permute-start | bytes 384008 | tf_op jit(solution)/shard_map/ppermute | solution.py:19
  157.1 1.0 fusion.29
  158.0 0.9 collective-permute-done.6
  159.0 5.9 %subtract_add_fusion.1 = f32[5,48,24,128]{3,2,1,0:T(8,128)S(1)} fusion(f32[5,48,24,128]{3,2,1,0:T(8,128)S(1)} %add.85, f32[5,48,24,127]{3,2,1,0:T(8,128)S(1)} %get-tuple-element.16, f32[5,48,24,127]{3,2,1,0:T(8,128)S(1)} %get-tuple-element.15, f32[5,1,24,128]{3,2,1,0:T(8,128)S(1)} %collective-permute-done, f32[5,1,24,128]{3,2,1,0:T(8,128)S(1)} %collective-permute-done.2, ...), kind=kLoop, calls=%fused_computation.32 | loop fusion | flops 25804800 | bytes 18027520 | tf_op jit(solution)/shard_map/add | solution.py:56
  164.9 1.2 collective-permute-start.9
  166.1 1.2 collective-permute-start.8
  167.3 2.3 %collective-permute-done.9 = f32[5,1,24,128]{3,2,1,0:T(8,128)S(1)} collective-permute-done((f32[5,1,24,128]{3,2,1,0:T(8,128)S(1)}, f32[5,1,24,128]{3,2,1,0:T(8,128)S(1)}, u32[]{:S(2)}, u32[]{:S(2)}) %collective-permute-start.9) | collective-permute-done | bytes 61472 | tf_op jit(solution)/shard_map/ppermute | solution.py:19
  170.3 2.4 %collective-permute-start.10 = (f32[5,50,1,128]{3,2,1,0:T(1,128)S(1)}, f32[5,50,1,128]{3,2,1,0:T(1,128)S(1)}, u32[]{:S(2)}, u32[]{:S(2)}) collective-permute-start(f32[5,50,1,128]{3,2,1,0:T(1,128)S(1)} %get-tuple-element.5), channel_id=1, source_target_pairs={{1,0},{2,1},{3,2},{4,3},{5,4},{6,5},{7,6},{9,8},{10,9},{11,10},{12... | collective-permute-start | bytes 384008 | tf_op jit(solution)/shard_map/ppermute | solution.py:22
  172.7 4.4 %collective-permute-start.11 = (f32[5,50,1,128]{3,2,1,0:T(1,128)S(1)}, f32[5,50,1,128]{3,2,1,0:T(1,128)S(1)}, u32[]{:S(2)}, u32[]{:S(2)}) collective-permute-start(f32[5,50,1,128]{3,2,1,0:T(1,128)S(1)} %get-tuple-element.6), channel_id=1, source_target_pairs={{0,1},{1,2},{2,3},{3,4},{4,5},{5,6},{6,7},{8,9},{9,10},{10,11},{11... | collective-permute-start | bytes 384008 | tf_op jit(solution)/shard_map/ppermute | solution.py:19
  177.1 1.0 fusion.27
  178.1 0.9 collective-permute-done.11
  179.0 6.8 %subtract_add_fusion = f32[5,48,24,128]{3,2,1,0:T(8,128)} fusion(f32[5,48,24,128]{3,2,1,0:T(8,128)S(1)} %subtract_add_fusion.1, f32[5,48,24,127]{3,2,1,0:T(8,128)S(1)} %get-tuple-element.12, f32[5,48,24,127]{3,2,1,0:T(8,128)S(1)} %get-tuple-element.11, f32[5,1,24,128]{3,2,1,0:T(8,128)S(1)} %collective-permute-done.8, ...), kind=kLoop, calls=%fused_computation.31 | loop fusion | flops 25804800 | bytes 18027520 | tf_op jit(solution)/shard_map/add | solution.py:56
  (54 shorter events, 5.9 us)
Async XLA Ops:
  6.5 23.9 %copy-start = (f32[3,48,24,128]{3,2,1,0:T(8,128)S(1)}, f32[3,48,24,128]{3,2,1,0:T(8,128)}, u32[]{:S(2)}) copy-start(f32[3,48,24,128]{3,2,1,0:T(8,128)} %param.15) | copy-start | bytes 5308420
  6.5 53.9 %all-gather.4.cloned.1.call-start = ((), (), s32[]{:S(2)}) async-start(), calls=%async_computation | async-start | bytes 4718592 | tf_op jit(solution)/shard_map/all_gather | solution.py:87
  10.8 35.0 %collective-permute-start.4 = (f32[3,1,24,128]{3,1,2,0:T(1,128)}, f32[3,1,24,128]{3,1,2,0:T(1,128)}, u32[]{:S(2)}, u32[]{:S(2)}) collective-permute-start(f32[3,1,24,128]{3,1,2,0:T(1,128)} %bitcast.14), channel_id=1, source_target_pairs={{8,0},{16,8},{24,16},{0,24},{9,1},{17,9},{25,17},{1,25},{10,2},{18... | collective-permute-start | bytes 110600 | tf_op jit(solution)/shard_map/ppermute | solution.py:22
  13.8 32.0 %collective-permute-start.1 = (f32[3,1,24,128]{3,1,2,0:T(1,128)}, f32[3,1,24,128]{3,1,2,0:T(1,128)}, u32[]{:S(2)}, u32[]{:S(2)}) collective-permute-start(f32[3,1,24,128]{3,1,2,0:T(1,128)} %bitcast.10), channel_id=1, source_target_pairs={{0,8},{8,16},{16,24},{24,0},{1,9},{9,17},{17,25},{25,1},{2,10},{10... | collective-permute-start | bytes 110600 | tf_op jit(solution)/shard_map/ppermute | solution.py:19
  46.5 7.2 %collective-permute-start.5 = (f32[3,50,1,128]{3,1,2,0:T(8,128)S(1)}, f32[3,50,1,128]{3,1,2,0:T(8,128)S(1)}, u32[]{:S(2)}, u32[]{:S(2)}) collective-permute-start(f32[3,50,1,128]{3,1,2,0:T(8,128)S(1)} %get-tuple-element.17), channel_id=1, source_target_pairs={{0,1},{1,2},{2,3},{3,4},{4,5},{5,6},{6,7},{8,9},{9,10},{10,11},{11... | collective-permute-start | bytes 230408 | tf_op jit(solution)/shard_map/ppermute | solution.py:19
  49.8 6.7 %collective-permute-start.7 = (f32[3,50,1,128]{3,1,2,0:T(8,128)S(1)}, f32[3,50,1,128]{3,1,2,0:T(8,128)S(1)}, u32[]{:S(2)}, u32[]{:S(2)}) collective-permute-start(f32[3,50,1,128]{3,1,2,0:T(8,128)S(1)} %get-tuple-element.18), channel_id=1, source_target_pairs={{1,0},{2,1},{3,2},{4,3},{5,4},{6,5},{7,6},{9,8},{10,9},{11,10},{12... | collective-permute-start | bytes 230408 | tf_op jit(solution)/shard_map/ppermute | solution.py:22
  53.7 4.1 %copy-start.8 = (f32[3,50,1,128]{3,1,2,0:T(8,128)}, f32[3,50,1,128]{3,1,2,0:T(8,128)S(1)}, u32[]{:S(2)}) copy-start(f32[3,50,1,128]{3,1,2,0:T(8,128)S(1)} %collective-permute-done.5) | copy-start | bytes 230404
  58.0 2.5 %copy-start.10 = (s32[1,1,8192]{2,1,0:T(1,128)S(1)}, s32[1,1,8192]{2,1,0:T(1,128)}, u32[]{:S(2)}) copy-start(s32[1,1,8192]{2,1,0:T(1,128)} %all-gather) | copy-start | bytes 98308
  58.0 2.5 %copy-start.11 = (f32[1,1,8192,1]{2,3,1,0:T(1,128)S(1)}, f32[1,1,8192,1]{2,3,1,0:T(1,128)}, u32[]{:S(2)}) copy-start(f32[1,1,8192,1]{2,3,1,0:T(1,128)} %compare_convert_fusion) | copy-start | bytes 98308
  60.4 70.4 %copy-start.12 = (s32[1,1,512]{2,1,0:T(1,128)S(1)}, s32[1,1,512]{2,1,0:T(1,128)}, u32[]{:S(2)}) copy-start(s32[1,1,512]{2,1,0:T(1,128)} %param.14) | copy-start | bytes 6148
  142.7 5.5 %copy-start.9 = (f32[3,50,1,128]{3,1,2,0:T(8,128)S(1)}, f32[3,50,1,128]{3,1,2,0:T(8,128)}, u32[]{:S(2)}) copy-start(f32[3,50,1,128]{3,1,2,0:T(8,128)} %copy-done.8) | copy-start | bytes 230404
  145.7 3.4 %copy-start.7 = (f32[48,24,128]{2,0,1:T(8,128)S(1)}, f32[48,24,128]{2,0,1:T(8,128)}, u32[]{:S(2)}) copy-start(f32[48,24,128]{2,0,1:T(8,128)} %get-tuple-element.24) | copy-start | bytes 1769476
  145.7 3.6 %copy-start.6 = (f32[48,24,128]{2,0,1:T(8,128)S(1)}, f32[48,24,128]{2,0,1:T(8,128)}, u32[]{:S(2)}) copy-start(f32[48,24,128]{2,0,1:T(8,128)} %get-tuple-element.25) | copy-start | bytes 1769476
  145.8 4.4 %collective-permute-start.2 = (f32[5,1,24,128]{3,2,1,0:T(8,128)S(1)}, f32[5,1,24,128]{3,2,1,0:T(8,128)S(1)}, u32[]{:S(2)}, u32[]{:S(2)}) collective-permute-start(f32[5,1,24,128]{3,2,1,0:T(8,128)S(1)} %get-tuple-element.13), channel_id=1, source_target_pairs={{0,8},{8,16},{16,24},{24,0},{1,9},{9,17},{17,25},{25,1},{2,10},{10... | collective-permute-start | bytes 184328 | tf_op jit(solution)/shard_map/ppermute | solution.py:19
  147.0 2.6 %copy-start.5 = (f32[48,24,128]{2,0,1:T(8,128)S(1)}, f32[48,24,128]{2,0,1:T(8,128)}, u32[]{:S(2)}) copy-start(f32[48,24,128]{2,0,1:T(8,128)} %get-tuple-element.26) | copy-start | bytes 1769476
  147.0 4.1 %collective-permute-start = (f32[5,1,24,128]{3,2,1,0:T(8,128)S(1)}, f32[5,1,24,128]{3,2,1,0:T(8,128)S(1)}, u32[]{:S(2)}, u32[]{:S(2)}) collective-permute-start(f32[5,1,24,128]{3,2,1,0:T(8,128)S(1)} %get-tuple-element.14), channel_id=1, source_target_pairs={{8,0},{16,8},{24,16},{0,24},{9,1},{17,9},{25,17},{1,25},{10,2},{18... | collective-permute-start | bytes 184328 | tf_op jit(solution)/shard_map/ppermute | solution.py:22
  149.0 1.1 copy-start.4
  151.3 6.7 %collective-permute-start.3 = (f32[5,50,1,128]{3,2,1,0:T(1,128)S(1)}, f32[5,50,1,128]{3,2,1,0:T(1,128)S(1)}, u32[]{:S(2)}, u32[]{:S(2)}) collective-permute-start(f32[5,50,1,128]{3,2,1,0:T(1,128)S(1)} %get-tuple-element.7), channel_id=1, source_target_pairs={{1,0},{2,1},{3,2},{4,3},{5,4},{6,5},{7,6},{9,8},{10,9},{11,10},{12... | collective-permute-start | bytes 384008 | tf_op jit(solution)/shard_map/ppermute | solution.py:22
  154.5 4.4 %copy-start.1 = (f32[48,24,128]{2,1,0:T(8,128)S(1)}, f32[48,24,128]{2,1,0:T(8,128)}, u32[]{:S(2)}) copy-start(f32[48,24,128]{2,1,0:T(8,128)} %get-tuple-element.19) | copy-start | bytes 1769476
  154.5 4.4 %copy-start.2 = (f32[48,24,128]{2,1,0:T(8,128)S(1)}, f32[48,24,128]{2,1,0:T(8,128)}, u32[]{:S(2)}) copy-start(f32[48,24,128]{2,1,0:T(8,128)} %get-tuple-element.20) | copy-start | bytes 1769476
  154.5 4.4 %copy-start.3 = (f32[48,24,128]{2,1,0:T(8,128)S(1)}, f32[48,24,128]{2,1,0:T(8,128)}, u32[]{:S(2)}) copy-start(f32[48,24,128]{2,1,0:T(8,128)} %get-tuple-element.21) | copy-start | bytes 1769476
  154.6 4.4 %collective-permute-start.6 = (f32[5,50,1,128]{3,2,1,0:T(1,128)S(1)}, f32[5,50,1,128]{3,2,1,0:T(1,128)S(1)}, u32[]{:S(2)}, u32[]{:S(2)}) collective-permute-start(f32[5,50,1,128]{3,2,1,0:T(1,128)S(1)} %get-tuple-element.8), channel_id=1, source_target_pairs={{0,1},{1,2},{2,3},{3,4},{4,5},{5,6},{6,7},{8,9},{9,10},{10,11},{11... | collective-permute-start | bytes 384008 | tf_op jit(solution)/shard_map/ppermute | solution.py:19
  164.9 4.7 %collective-permute-start.9 = (f32[5,1,24,128]{3,2,1,0:T(8,128)S(1)}, f32[5,1,24,128]{3,2,1,0:T(8,128)S(1)}, u32[]{:S(2)}, u32[]{:S(2)}) collective-permute-start(f32[5,1,24,128]{3,2,1,0:T(8,128)S(1)} %get-tuple-element.9), channel_id=1, source_target_pairs={{0,8},{8,16},{16,24},{24,0},{1,9},{9,17},{17,25},{25,1},{2,10},{10... | collective-permute-start | bytes 184328 | tf_op jit(solution)/shard_map/ppermute | solution.py:19
  166.1 4.0 %collective-permute-start.8 = (f32[5,1,24,128]{3,2,1,0:T(8,128)S(1)}, f32[5,1,24,128]{3,2,1,0:T(8,128)S(1)}, u32[]{:S(2)}, u32[]{:S(2)}) collective-permute-start(f32[5,1,24,128]{3,2,1,0:T(8,128)S(1)} %get-tuple-element.10), channel_id=1, source_target_pairs={{8,0},{16,8},{24,16},{0,24},{9,1},{17,9},{25,17},{1,25},{10,2},{18... | collective-permute-start | bytes 184328 | tf_op jit(solution)/shard_map/ppermute | solution.py:22
  170.3 7.8 %collective-permute-start.10 = (f32[5,50,1,128]{3,2,1,0:T(1,128)S(1)}, f32[5,50,1,128]{3,2,1,0:T(1,128)S(1)}, u32[]{:S(2)}, u32[]{:S(2)}) collective-permute-start(f32[5,50,1,128]{3,2,1,0:T(1,128)S(1)} %get-tuple-element.5), channel_id=1, source_target_pairs={{1,0},{2,1},{3,2},{4,3},{5,4},{6,5},{7,6},{9,8},{10,9},{11,10},{12... | collective-permute-start | bytes 384008 | tf_op jit(solution)/shard_map/ppermute | solution.py:22
  172.7 6.3 %collective-permute-start.11 = (f32[5,50,1,128]{3,2,1,0:T(1,128)S(1)}, f32[5,50,1,128]{3,2,1,0:T(1,128)S(1)}, u32[]{:S(2)}, u32[]{:S(2)}) collective-permute-start(f32[5,50,1,128]{3,2,1,0:T(1,128)S(1)} %get-tuple-element.6), channel_id=1, source_target_pairs={{0,1},{1,2},{2,3},{3,4},{4,5},{5,6},{6,7},{8,9},{9,10},{10,11},{11... | collective-permute-start | bytes 384008 | tf_op jit(solution)/shard_map/ppermute | solution.py:19
Sparse Core Ops, SparseCore 0:
  9.5 50.8 all-gather.3
where the time goes:
time: 193 us
  matrix products  77.5 us (40%)
  blocking collectives  30.3 us (16%)
  starting transfers between devices  25.5 us (13%)
  other arithmetic  25.5 us (13%)
  between operations  14.5 us (8%)
  local copies, waits for them, and re-layouts  10.1 us (5%)
  waiting for transfers between devices  9.26 us (5%)
    dot_general x1, matrix products, station_sums(): jnp.dot(selector, amounts, precision=lax.Precision.HIGHEST, preferred_ele...  70.4 us
    all_gather x1, blocking collectives, body(): piece_bands = lax.all_gather(bands, 'lat', axis=0, tiled=True)  15.3 us
    all_gather x1, blocking collectives, body(): piece_codes = lax.all_gather(codes, 'lat', axis=0, tiled=True)  15 us
    ppermute x6, starting transfers between devices, padded_2(): lax.ppermute(lax.slice_in_dim(block, 0, width, axis=dim), axis, backward)  13 us
    add x2, other arithmetic, advance(): return centre + ADVECT_SCALE * transport + mixing  12.7 us
    ppermute x6, starting transfers between devices, padded_2(): lax.ppermute(lax.slice_in_dim(block, block.shape[dim] - width, None, axis...  12.5 us
    dot_general x1, matrix products, body(): jnp.einsum('cs,vsl->vcl', cell_map, sums.reshape(var_count, STATIONS, lev...  7.04 us
    transpose x1, local copies, waits for them, and re-layouts, body(): jnp.einsum('cs,vsl->vcl', cell_map, sums.reshape(var_count, STATIONS, lev...  4.76 us
  transfers between devices with their start and end apart: 13, of which 7 were waited for; matrix products, arithmetic and copies ran while one was open for 6% of the time, Pallas kernels for 0%

commit v1 on v0

v1 whole, which is shorter than its diff:
```python
import functools

import jax
import jax.numpy as jnp
from jax import lax
from jax.experimental import pallas as pl
from jax.experimental.pallas import tpu as pltpu
from jax.sharding import PartitionSpec as P

ADVECT_SCALE = 0.2
LANES = 128
STRIDE = 1024
HEADER = 8
VMEM_LIMIT = 40 * 1024 * 1024
V = pltpu.VMEM


def in_vmem(array):
    return pltpu.with_memory_space_constraint(array, V)


def in_hbm(array):
    return pltpu.with_memory_space_constraint(array, pltpu.HBM)


def params():
    return pltpu.CompilerParams(vmem_limit_bytes=VMEM_LIMIT)


def start_all(copies):
    for copy in copies:
        copy.start()


def wait_all(copies):
    for copy in copies:
        copy.wait()


def run(copies):
    start_all(copies)
    wait_all(copies)


def pack_kernel(
    n, cap, stations, count_ref, band_ref, station_ref, var_ref, dep_ref, coef_ref, *rest
):
    half = n // 2
    own, swap = rest[:2]
    through = rest[2 : half + 1]
    south, north = rest[half + 1 : half + 3]
    (dep, band, station, var, low, high, buf, pos_v, pos_s, sem) = rest[half + 3 :]
    me = lax.axis_index("lat")
    rows, lanes = band.shape
    lat_cells = coef_ref.shape[2]
    loads = [
        pltpu.make_async_copy(src, dst, sem.at[k])
        for k, (src, dst) in enumerate(
            (
                (band_ref, band),
                (station_ref, station),
                (var_ref, var),
                (dep_ref, dep),
                (coef_ref.at[:, :, pl.ds(0, 8)], low),
                (coef_ref.at[:, :, pl.ds(lat_cells - 8, 8)], high),
            )
        )
    ]
    start_all(loads)
    wait_all(loads[:3])
    count = count_ref[0, 0]
    slot = (
        lax.broadcasted_iota(jnp.int32, (rows, lanes), 0) * lanes
        + lax.broadcasted_iota(jnp.int32, (rows, lanes), 1)
    )
    far = (band[...] >> 1) - (me >> 1)
    far = jnp.where(far < 0, far + half, far)
    group = jnp.where((band[...] & 1) == (me & 1), far, far + half)
    group = jnp.where(slot < count, group, n)
    masks = jnp.concatenate([(group == s).astype(jnp.float32) for s in range(n)], axis=0)
    before = lax.broadcasted_iota(jnp.int32, (lanes, lanes), 0) < lax.broadcasted_iota(
        jnp.int32, (lanes, lanes), 1
    )
    prefix = jnp.dot(masks, before.astype(jnp.float32), preferred_element_type=jnp.float32)
    totals = jnp.dot(
        masks, jnp.ones((lanes, lanes), jnp.float32), preferred_element_type=jnp.float32
    )
    a = lax.broadcasted_iota(jnp.int32, (rows * n, rows * n), 0)
    b = lax.broadcasted_iota(jnp.int32, (rows * n, rows * n), 1)
    earlier = ((a // rows == b // rows) & (b < a)).astype(jnp.float32)
    offset = jnp.dot(earlier, totals, preferred_element_type=jnp.float32)
    ranks = (prefix + offset).astype(jnp.int32)
    rank = jnp.zeros((rows, lanes), jnp.int32)
    for s in range(n):
        rank = jnp.where(group == s, ranks[s * rows : (s + 1) * rows], rank)
    pos_v[...] = group * STRIDE + rank
    place_map = pltpu.make_async_copy(pos_v, pos_s, sem.at[0])
    place_map.start()
    code = var[...] * stations + station[...]
    upper = (code >> 6).astype(jnp.float32)
    lower = (code & 63).astype(jnp.float32)
    width = -(-cap // lanes) * lanes
    which = lax.broadcasted_iota(jnp.int32, (n, lanes), 0)
    order = lax.broadcasted_iota(jnp.int32, (width, lanes), 0)
    codes = jnp.zeros((2 * n, width), jnp.float32)
    for k in range(rows):
        mine = which == group[k : k + 1]
        parts = jnp.concatenate(
            [jnp.where(mine, upper[k : k + 1], 0.0), jnp.where(mine, lower[k : k + 1], 0.0)], 0
        )
        codes += lax.dot_general(
            parts,
            (order == rank[k : k + 1]).astype(jnp.float32),
            (((1,), (1,)), ((), ())),
            preferred_element_type=jnp.float32,
        )
    codes = codes[:n] * 64.0 + codes[n:]
    counts = offset + totals
    size = cap + HEADER

    def target(s):
        if s == 0:
            return own, 0
        if s < half:
            return through[s - 1], 0
        return swap, (s - half) * size

    for s in range(n):
        to, at = target(s)
        for j in range(width // lanes):
            to[pl.ds(at + cap + j, 1), :] = codes[s : s + 1, j * lanes : (j + 1) * lanes]
        to[pl.ds(at + cap + HEADER - 1, 1), :] = counts[(s + 1) * rows - 1 : (s + 1) * rows]
    wait_all(loads[3:])
    fields, lons = low.shape[:2]

    def strip(i, carry):
        for f in range(fields):
            north[pl.ds((f * lons + i) * 2, 2), :] = high[f, i, 6:8]
            south[pl.ds((f * lons + i) * 2, 2), :] = low[f, i, 0:2]
        return carry

    lax.fori_loop(0, lons, strip, 0)
    place_map.wait()

    def place(g, carry):
        base = pl.multiple_of(g * 16, 16)
        row, col = base >> 7, base & 127
        for k in range(16):
            buf[pl.ds(pos_s[row, col + k], 1), :] = dep[pl.ds(base + k, 1), :]
        return carry

    lax.fori_loop(0, (count + 15) >> 4, place, 0)
    for s in range(n):
        to, at = target(s)
        to[pl.ds(at, cap), :] = buf[pl.ds(s * STRIDE, cap), :]


def pack(n, cap, stations, count, band, station, var, dep, coef):
    rows = dep.shape[0] // LANES
    fields, lons = coef.shape[:2]
    size, half = cap + HEADER, n // 2
    strip = (fields * lons * 2, LANES)
    shapes = [(size, LANES), (half * size, LANES)]
    shapes += [(2 * size, LANES)] * (half - 1) + [strip, strip]
    hbm = pl.BlockSpec(memory_space=pltpu.HBM)
    vm = pl.BlockSpec(memory_space=V)
    return pl.pallas_call(
        functools.partial(pack_kernel, n, cap, stations),
        out_shape=tuple(V(shape, jnp.float32) for shape in shapes),
        in_specs=[pl.BlockSpec(memory_space=pltpu.SMEM)] + [hbm] * 5,
        out_specs=(vm,) * len(shapes),
        scratch_shapes=[
            V(dep.shape, jnp.float32),
            V((rows, LANES), jnp.int32),
            V((rows, LANES), jnp.int32),
            V((rows, LANES), jnp.int32),
            V((fields, lons, 8, LANES), jnp.float32),
            V((fields, lons, 8, LANES), jnp.float32),
            V((n * STRIDE + HEADER + STRIDE, LANES), jnp.float32),
            V((rows, LANES), jnp.int32),
            pltpu.SMEM((rows, LANES), jnp.int32),
            pltpu.SemaphoreType.DMA((6,)),
        ],
        compiler_params=params(),
        name="pack",
    )(count, *(in_hbm(array) for array in (band, station, var, dep, coef)))


def relay_kernel(k, size, swapped, *rest):
    for j, to in enumerate(rest[k:]):
        to[pl.ds(size, size), :] = swapped[pl.ds((j + 1) * size, size), :]


def relay(swapped, through, size):
    k = len(through)
    vm = pl.BlockSpec(memory_space=V)
    return pl.pallas_call(
        functools.partial(relay_kernel, k, size),
        out_shape=tuple(V(array.shape, jnp.float32) for array in through),
        in_specs=[vm] * (k + 1),
        out_specs=(vm,) * k,
        input_output_aliases={j + 1: j for j in range(k)},
        compiler_params=params(),
        name="relay",
    )(in_vmem(swapped), *(in_vmem(array) for array in through))


def open_header(packet, base, cap, view, header, sem):
    view[...] = packet[pl.ds(base + cap, HEADER), :].astype(jnp.int32)
    copy = pltpu.make_async_copy(view, header, sem)
    copy.start()
    return copy


def scatter_packet(table_ref, packet, start, header, state):
    unroll = 8
    count = header[HEADER - 1, 0]

    def some(g, carry):
        base = g * unroll
        major, minor = base >> 7, base & 127
        rows = [table_ref[0, header[major, minor + k]] for k in range(unroll)]
        for k in range(unroll):
            state[pl.ds(rows[k], 1), :] += packet[pl.ds(start + base + k, 1), :]
        return carry

    def one(j, carry):
        row = table_ref[0, header[j >> 7, j & 127]]
        state[pl.ds(row, 1), :] += packet[pl.ds(start + j, 1), :]
        return carry

    whole = count >> 3
    lax.fori_loop(0, whole, some, 0)
    lax.fori_loop(whole * unroll, count, one, 0)


def first_kernel(
    lons, lats, cap, table_ref, adjoint_ref, own_ref, swap_ref, state, full, *rest
):
    views, headers, sem = rest[:2], rest[2:4], rest[4]
    span = lats + 4
    ring = (lons + 4) * span
    nv = state.shape[0] // ring
    load = pltpu.make_async_copy(adjoint_ref, full, sem.at[0])
    load.start()
    packets = (own_ref, swap_ref)
    opened = [
        open_header(packets[j], 0, cap, views[j], headers[j], sem.at[j + 1]) for j in range(2)
    ]
    load.wait()

    def fill(i, carry):
        for v in range(nv):
            to = v * ring + (i + 2) * span + 2
            at = (v * lons + i) * lats
            for r in range(0, lats, 8):
                state[pl.ds(to + r, 8), :] = full[pl.ds(pl.multiple_of(at + r, 8), 8), :]
        return carry

    lax.fori_loop(0, lons, fill, 0)
    wait_all(opened)
    for j in range(2):
        scatter_packet(table_ref, packets[j], 0, headers[j], state)


def scatter_first(table, adjoint, own, swapped, cap, shape):
    nv, lons, lats = shape
    hbm = pl.BlockSpec(memory_space=pltpu.HBM)
    ring = (lons + 4) * (lats + 4)
    return pl.pallas_call(
        functools.partial(first_kernel, lons, lats, cap),
        out_shape=V((nv * ring, LANES), jnp.float32),
        in_specs=[pl.BlockSpec(memory_space=pltpu.SMEM), hbm] + [pl.BlockSpec(memory_space=V)] * 2,
        out_specs=pl.BlockSpec(memory_space=V),
        scratch_shapes=[
            V(adjoint.shape, jnp.float32),
            V((HEADER, LANES), jnp.int32),
            V((HEADER, LANES), jnp.int32),
            pltpu.SMEM((HEADER, LANES), jnp.int32),
            pltpu.SMEM((HEADER, LANES), jnp.int32),
            pltpu.SemaphoreType.DMA((3,)),
        ],
        compiler_params=params(),
        name="scatter_own",
    )(table, in_hbm(adjoint), in_vmem(own), in_vmem(swapped))


def more_kernel(k, lons, lats, cap, last, table_ref, *rest):
    packets = [(rest[j], base) for j in range(k) for base in (0, cap + HEADER)]
    m = len(packets)
    rest = rest[len(rest) - (3 if last else 1) - 2 * m - 1 :]
    outs, rest = rest[: 3 if last else 1], rest[3 if last else 1 :]
    views, headers, sem = rest[:m], rest[m : 2 * m], rest[2 * m]
    state = outs[0]
    opened = [
        open_header(*packets[j], cap, views[j], headers[j], sem.at[j]) for j in range(m)
    ]
    wait_all(opened)
    for j in range(m):
        scatter_packet(table_ref, *packets[j], headers[j], state)
    if not last:
        return
    south, north = outs[1:]
    span = lats + 4
    ring = (lons + 4) * span
    nv = state.shape[0] // ring

    def strip(i, carry):
        for v in range(nv):
            at = v * ring + (i + 2) * span
            to = (v * lons + i) * 2
            south[pl.ds(to, 2), :] = state[pl.ds(at + 2, 2), :]
            north[pl.ds(to, 2), :] = state[pl.ds(at + lats, 2), :]
        return carry

    lax.fori_loop(0, lons, strip, 0)


def scatter_more(table, state, packets, cap, shape, last, after=()):
    nv, lons, lats = shape
    k = len(packets)
    vm = pl.BlockSpec(memory_space=V)
    out = V(state.shape, jnp.float32)
    strip = V((nv * lons * 2, LANES), jnp.float32)
    return pl.pallas_call(
        functools.partial(more_kernel, k, lons, lats, cap, last),
        out_shape=(out, strip, strip) if last else out,
        in_specs=[pl.BlockSpec(memory_space=pltpu.SMEM)] + [vm] * (k + 1 + len(after)),
        out_specs=(vm, vm, vm) if last else vm,
        input_output_aliases={k + 1: 0},
        scratch_shapes=[V((HEADER, LANES), jnp.int32)] * (2 * k)
        + [pltpu.SMEM((HEADER, LANES), jnp.int32)] * (2 * k)
        + [pltpu.SemaphoreType.DMA((2 * k,))],
        compiler_params=params(),
        name="scatter_last" if last else "scatter_more",
    )(
        table,
        *(in_vmem(packet) for packet in packets),
        in_vmem(state),
        *(in_vmem(array) for array in after),
    )


def widen_kernel(coef_ref, south_ref, north_ref, ring_out, west, east, own, sem):
    fields, lons, lats, _ = coef_ref.shape
    span = lats + 4
    ring = (lons + 4) * span
    me = lax.axis_index("lat")
    has_south = (me > 0).astype(jnp.float32)
    has_north = (me < lax.axis_size("lat") - 1).astype(jnp.float32)
    run([pltpu.make_async_copy(coef_ref, own, sem)])

    def fill(i, carry):
        for f in range(fields):
            to = f * ring + (i + 2) * span
            at = (f * lons + i) * 2
            for r in range(0, lats, 8):
                ring_out[pl.ds(to + 2 + r, 8), :] = own[f, i, r : r + 8]
            ring_out[pl.ds(to, 2), :] = south_ref[pl.ds(at, 2), :] * has_south
            ring_out[pl.ds(to + lats + 2, 2), :] = north_ref[pl.ds(at, 2), :] * has_north
        return carry

    lax.fori_loop(0, lons, fill, 0)
    for f in range(fields):
        west[pl.ds(f * 2 * span, 2 * span), :] = ring_out[pl.ds(f * ring + 2 * span, 2 * span), :]
        east[pl.ds(f * 2 * span, 2 * span), :] = ring_out[
            pl.ds(f * ring + lons * span, 2 * span), :
        ]


def widen(coef, south, north):
    fields, lons, lats, _ = coef.shape
    span = lats + 4
    vm = pl.BlockSpec(memory_space=V)
    edge = V((fields * 2 * span, LANES), jnp.float32)
    return pl.pallas_call(
        widen_kernel,
        out_shape=(V((fields * (lons + 4) * span, LANES), jnp.float32), edge, edge),
        in_specs=[pl.BlockSpec(memory_space=pltpu.HBM), vm, vm],
        out_specs=(vm, vm, vm),
        scratch_shapes=[V(coef.shape, jnp.float32), pltpu.SemaphoreType.DMA],
        compiler_params=params(),
        name="widen",
    )(in_hbm(coef), in_vmem(south), in_vmem(north))


def combine_kernel(lons, lats, ring_ref, west, east, out_ref, field):
    me = lax.axis_index("lat")
    total = lats * lax.axis_size("lat")
    span, rim = lats + 4, lats + 2
    ring = (lons + 4) * span
    size = rim_rows(lons, lats)
    field[...] = ring_ref[...]
    for f in range(field.shape[0] // ring):
        field[pl.ds(f * ring, 2 * span), :] = west[pl.ds(f * 2 * span, 2 * span), :]
        field[pl.ds(f * ring + (lons + 2) * span, 2 * span), :] = east[
            pl.ds(f * 2 * span, 2 * span), :
        ]
    lev = lax.broadcasted_iota(jnp.int32, (8, LANES), 1)
    row = lax.broadcasted_iota(jnp.int32, (8, LANES), 0)

    def one(i, carry):
        for r in chunks(rim):
            lat = row + (r - 1) + me * lats
            inside = (lat >= 0) & (lat < total)
            at = (i + 1) * span + r + 1

            def wind(f, shift, at=at):
                return ADVECT_SCALE * field[pl.ds(f * ring + at + shift, 8), :]

            def half(shift, at=at):
                return 0.5 * field[pl.ds(2 * ring + at + shift, 8), :]

            mine = half(0)
            east_factor = wind(0, 0) + (mine + half(span))
            west_factor = (mine + half(-span)) - wind(0, -span)
            north_factor = wind(1, 0) + (mine + half(1))
            south_factor = (mine + half(-1)) - wind(1, -1)
            up = jnp.where(lev < LANES - 1, mine + pltpu.roll(mine, LANES - 1, 1), 0.0)
            down = jnp.where(lev > 0, mine + pltpu.roll(mine, 1, 1), 0.0)
            centre = 1.0 - (
                ((east_factor + west_factor) + (north_factor + south_factor)) + (up + down)
            )
            factors = (centre, east_factor, west_factor, north_factor, south_factor, up, down)
            for k, value in enumerate(factors):
                out_ref[pl.ds(k * size + i * rim + r, 8), :] = jnp.where(inside, value, 0.0)
        return carry

    lax.fori_loop(0, lons + 2, one, 0)


def combine(ring, west, east, lons, lats):
    vm = pl.BlockSpec(memory_space=V)
    return pl.pallas_call(
        functools.partial(combine_kernel, lons, lats),
        out_shape=V((7 * rim_rows(lons, lats), LANES), jnp.float32),
        in_specs=[vm, vm, vm],
        out_specs=vm,
        scratch_shapes=[V(ring.shape, jnp.float32)],
        compiler_params=params(),
        name="combine",
    )(in_vmem(ring), in_vmem(west), in_vmem(east))


def rim_rows(lons, lats):
    return -(-(lons + 2) * (lats + 2) // 8) * 8


def chunks(rows):
    starts = list(range(0, rows - 7, 8))
    if starts[-1] + 8 < rows:
        starts.append(rows - 8)
    return starts


def weighted(factors, source, at, east):
    centre = source[pl.ds(at, 8), :]
    total = factors[0] * centre + factors[1] * source[pl.ds(at + east, 8), :]
    other = factors[2] * source[pl.ds(at - east, 8), :] + factors[3] * source[pl.ds(at + 1, 8), :]
    third = factors[4] * source[pl.ds(at - 1, 8), :] + factors[5] * pltpu.roll(
        centre, LANES - 1, 1
    )
    return (total + other) + (third + factors[6] * pltpu.roll(centre, 1, 1))


def first_step(coef_ref, state, mid, nv, lons, lats, i):
    span, rim = lats + 4, lats + 2
    ring, size = (lons + 4) * span, rim_rows(lons, lats)
    for r in chunks(rim):
        factors = [coef_ref[pl.ds(k * size + i * rim + r, 8), :] for k in range(7)]
        for v in range(nv):
            mid[pl.ds(v * size + i * rim + r, 8), :] = weighted(
                factors, state, v * ring + (i + 1) * span + r + 1, span
            )


def second_step(coef_ref, mid, out, nv, lons, lats, i, place):
    rim = lats + 2
    size = rim_rows(lons, lats)
    for r in range(0, lats, 8):
        at = (i + 1) * rim + r + 1
        factors = [coef_ref[pl.ds(k * size + at, 8), :] for k in range(7)]
        for v in range(nv):
            out[pl.ds(pl.multiple_of(place(v) + r, 8), 8), :] = weighted(
                factors, mid, v * size + at, rim
            )


def insert_kernel(lons, lats, state_in, south, north, state, west, east):
    span = lats + 4
    ring = (lons + 4) * span
    nv = state.shape[0] // ring

    def strip(i, carry):
        for v in range(nv):
            at = v * ring + (i + 2) * span
            frm = (v * lons + i) * 2
            state[pl.ds(at, 2), :] = south[pl.ds(frm, 2), :]
            state[pl.ds(at + lats + 2, 2), :] = north[pl.ds(frm, 2), :]
        return carry

    lax.fori_loop(0, lons, strip, 0)
    for v in range(nv):
        west[pl.ds(v * 2 * span, 2 * span), :] = state[pl.ds(v * ring + 2 * span, 2 * span), :]
        east[pl.ds(v * 2 * span, 2 * span), :] = state[pl.ds(v * ring + lons * span, 2 * span), :]


def insert(state, south, north, shape):
    nv, lons, lats = shape
    vm = pl.BlockSpec(memory_space=V)
    edge = V((nv * 2 * (lats + 4), LANES), jnp.float32)
    return pl.pallas_call(
        functools.partial(insert_kernel, lons, lats),
        out_shape=(V(state.shape, jnp.float32), edge, edge),
        in_specs=[vm] * 3,
        out_specs=(vm,) * 3,
        input_output_aliases={0: 0},
        compiler_params=params(),
        name="insert",
    )(in_vmem(state), in_vmem(south), in_vmem(north))


def inner_kernel(lons, lats, coef_ref, state, mid, out_ref, out, sem):
    nv = out.shape[0] // (lons * lats)
    cells = lons * lats

    def first(i, carry):
        first_step(coef_ref, state, mid, nv, lons, lats, i)
        return carry

    lax.fori_loop(2, lons, first, 0)

    def second(i, carry):
        second_step(
            coef_ref, mid, out, nv, lons, lats, i, lambda v: v * cells + i * lats
        )
        return carry

    parts = 4
    edges = [2 + (lons - 4) * p // parts for p in range(parts + 1)]
    copies = []
    for p in range(parts):
        lax.fori_loop(edges[p], edges[p + 1], second, 0)
        for v in range(nv):
            span = pl.ds(v * cells + edges[p] * lats, (edges[p + 1] - edges[p]) * lats)
            copy = pltpu.make_async_copy(out.at[span], out_ref.at[span], sem.at[p * nv + v])
            copy.start()
            copies.append(copy)
    wait_all(copies)


def inner(coef, state, shape):
    nv, lons, lats = shape
    vm = pl.BlockSpec(memory_space=V)
    return pl.pallas_call(
        functools.partial(inner_kernel, lons, lats),
        out_shape=(
            V((nv * rim_rows(lons, lats), LANES), jnp.float32),
            jax.ShapeDtypeStruct((nv * lons * lats, LANES), jnp.float32),
        ),
        in_specs=[vm, vm],
        out_specs=(vm, pl.BlockSpec(memory_space=pltpu.HBM)),
        scratch_shapes=[
            V((nv * lons * lats, LANES), jnp.float32),
            pltpu.SemaphoreType.DMA((4 * nv,)),
        ],
        compiler_params=params(),
        name="inner",
    )(in_vmem(coef), in_vmem(state))


def outer_kernel(
    lons, lats, coef_ref, state_in, mid_in, west, east, out_in, state, mid, out_ref, out, sem
):
    span = lats + 4
    ring = (lons + 4) * span
    nv = state.shape[0] // ring
    cells = lons * lats
    for v in range(nv):
        state[pl.ds(v * ring, 2 * span), :] = west[pl.ds(v * 2 * span, 2 * span), :]
        state[pl.ds(v * ring + (lons + 2) * span, 2 * span), :] = east[
            pl.ds(v * 2 * span, 2 * span), :
        ]

    def first(k, carry):
        i = jnp.where(k < 2, k, lons - 2 + k)
        first_step(coef_ref, state, mid, nv, lons, lats, i)
        return carry

    lax.fori_loop(0, 4, first, 0)

    def second(k, carry):
        i = jnp.where(k < 2, k, lons - 4 + k)
        second_step(
            coef_ref, mid, out, nv, lons, lats, i, lambda v: (v * 4 + k) * lats
        )
        return carry

    lax.fori_loop(0, 4, second, 0)
    copies = []
    for v in range(nv):
        for side, at in ((0, 0), (1, lons - 2)):
            copies.append(
                pltpu.make_async_copy(
                    out.at[pl.ds((v * 4 + 2 * side) * lats, 2 * lats)],
                    out_ref.at[pl.ds(v * cells + at * lats, 2 * lats)],
                    sem.at[v * 2 + side],
                )
            )
    run(copies)


def outer(coef, state, mid, west, east, out, shape):
    nv, lons, lats = shape
    vm = pl.BlockSpec(memory_space=V)
    hbm = pl.BlockSpec(memory_space=pltpu.HBM)
    return pl.pallas_call(
        functools.partial(outer_kernel, lons, lats),
        out_shape=(
            V(state.shape, jnp.float32),
            V(mid.shape, jnp.float32),
            jax.ShapeDtypeStruct(out.shape, jnp.float32),
        ),
        in_specs=[vm] * 5 + [hbm],
        out_specs=(vm, vm, hbm),
        input_output_aliases={1: 0, 2: 1, 5: 2},
        scratch_shapes=[V((nv * 4 * lats, LANES), jnp.float32), pltpu.SemaphoreType.DMA((2 * nv,))],
        compiler_params=params(),
        name="outer",
    )(in_vmem(coef), in_vmem(state), in_vmem(mid), in_vmem(west), in_vmem(east), out)[2]


def from_sides(low_part, high_part, axis, periodic):
    count = lax.axis_size(axis)
    forward = [(i, i + 1) for i in range(count - 1)]
    if periodic:
        forward.append((count - 1, 0))
    backward = [(target, source) for source, target in forward]
    return lax.ppermute(high_part, axis, forward), lax.ppermute(low_part, axis, backward)


def body(
    adjoint_in, departures, obs_band, obs_station, obs_var, counts, station_cell, coefficients
):
    nv, lons, lats, levels = adjoint_in.shape
    shape = (nv, lons, lats)
    slots = departures.shape[2]
    n = lax.axis_size("lat")
    cap = -(-3 * slots // n // 8) * 8
    stations = station_cell.shape[2]
    square = (slots // LANES, LANES)
    own, swap, *rest = pack(
        n,
        cap,
        stations,
        counts,
        obs_band.reshape(square),
        obs_station.reshape(square),
        obs_var.reshape(square),
        departures.reshape(slots, levels),
        coefficients,
    )
    through, (south, north) = rest[:-2], rest[-2:]
    swapped = lax.ppermute(swap, "lat", [(i, i ^ 1) for i in range(n)])
    south, north = from_sides(south, north, "lat", False)
    through = relay(swapped, through, cap + HEADER)
    order = sorted(range(1, n // 2), key=lambda s: abs(4 * s - n))
    moved = [
        lax.ppermute(through[s - 1], "lat", [(i, (i + 2 * s) % n) for i in range(n)])
        for s in order
    ]
    cell = station_cell.reshape(1, stations)
    span = lats + 4
    spot = (cell // lats + 2) * span + cell % lats + 2
    tile = (lons + 4) * span
    table = jnp.concatenate([spot + v * tile for v in range(nv)], axis=1)
    state = scatter_first(
        table, adjoint_in.reshape(nv * lons * lats, levels), own, swapped, cap, shape
    )
    ring, west, east = widen(coefficients, south, north)
    west, east = from_sides(west, east, "lon", True)
    coef = combine(ring, west, east, lons, lats)
    state = scatter_more(table, state, moved[:1], cap, shape, False, (coef,))
    state, south, north = scatter_more(table, state, moved[1:], cap, shape, True)
    south, north = from_sides(south, north, "lat", False)
    state, west, east = insert(state, south, north, shape)
    west, east = from_sides(west, east, "lon", True)
    mid, out = inner(coef, state, shape)
    out = outer(coef, state, mid, west, east, out, shape)
    return out.reshape(adjoint_in.shape)


def solution(mesh):
    in_specs = (
        P(None, "lon", "lat", None),
        P("lon", "lat", None, None),
        P("lon", "lat", None, None),
        P("lon", "lat", None),
        P("lon", "lat", None),
        P("lon", "lat"),
        P("lon", "lat", None),
        P(None, "lon", "lat", None),
    )
    out_specs = P(None, "lon", "lat", None)
    return jax.shard_map(body, mesh=mesh, in_specs=in_specs, out_specs=out_specs, check_vma=False)
```

time: 193 us -> 85.3 us (0.44)
  the two profiles are of different devices: /device:TPU:1 before, /device:TPU:17 now
where the time goes in v1:
time: 85.3 us; the launch traced here: 84.7 us
  Pallas kernels  32.2 us (38%)
  waiting for transfers between devices  28.5 us (33%)
  starting transfers between devices  22.4 us (26%)
    ppermute x3, waiting for transfers between devices, body(): lax.ppermute(through[s - 1], 'lat', [(i, (i + 2 * s) % n) for i in range(...  13.8 us
    ppermute x4, starting transfers between devices, from_sides(): lax.ppermute(high_part, axis, forward)  11.4 us
    pallas_call x1, Pallas kernels, inner(): pl.pallas_call(functools.partial(inner_kernel, lons, lats), out_shape=(V(...  11 us
    ppermute x4, waiting for transfers between devices, from_sides(): lax.ppermute(low_part, axis, backward)  10.8 us
    ppermute x4, starting transfers between devices, from_sides(): lax.ppermute(low_part, axis, backward)  7.54 us
    pallas_call x2, Pallas kernels, scatter_more(): pl.pallas_call(functools.partial(more_kernel, k, lons, lats, cap, last),...  5.34 us
    pallas_call x1, Pallas kernels, combine(): pl.pallas_call(functools.partial(combine_kernel, lons, lats), out_shape=V...  4.3 us
    pallas_call x1, Pallas kernels, pack(): pl.pallas_call(functools.partial(pack_kernel, n, cap, stations), out_shap...  4.07 us
  transfers between devices with their start and end apart: 12, of which 6 were waited for; matrix products, arithmetic and copies ran while one was open for 1% of the time, Pallas kernels for 27%

profile of v1, /device:TPU:17, one launch (start us, length us, event | category | flops | bytes accessed | tf_op | source)
XLA Modules:
  0.0 84.7 jit_solution(10617114366320285745)
XLA Ops:
  0.7 4.1 %pack.1 = (f32[392,128]{1,0:T(8,128)S(1)}, f32[1568,128]{1,0:T(8,128)S(1)}, f32[784,128]{1,0:T(8,128)S(1)}, f32[784,128]{1,0:T(8,128)S(1)}, f32[784,128]{1,0:T(8...) custom-call(s32[1,1]{1,0:T(1,128)S(6)} %copy.31.count_ref, s32[8,128]{1,0:T(8,128)} %bitcast.26, ...), custom_call_target="tpu_custom_call" | custom-call | tf_op jit(solution)/shard_map/pack/pallas_call | solution.py:167
  4.7 0.4 collective-permute-start.4
  5.2 3.6 %collective-permute-start = (f32[288,128]{1,0:T(8,128)S(1)}, f32[288,128]{1,0:T(8,128)S(1)}, u32[]{:S(2)}, u32[]{:S(2)}) collective-permute-start(f32[288,128]{1,0:T(8,128)S(1)} %get-tuple-element.27), channel_id=1, source_target_pairs={{0,1},{1,2},{2,3},{3,4},{4,5},{5,6},{6,7},{8,9},{9,10},{10,11},{11... | collective-permute-start | bytes 442376 | tf_op jit(solution)/shard_map/ppermute | solution.py:639
  8.7 1.9 %collective-permute-start.1 = (f32[288,128]{1,0:T(8,128)S(1)}, f32[288,128]{1,0:T(8,128)S(1)}, u32[]{:S(2)}, u32[]{:S(2)}) collective-permute-start(f32[288,128]{1,0:T(8,128)S(1)} %get-tuple-element.28), channel_id=1, source_target_pairs={{1,0},{2,1},{3,2},{4,3},{5,4},{6,5},{7,6},{9,8},{10,9},{11,10},{12... | collective-permute-start | bytes 442376 | tf_op jit(solution)/shard_map/ppermute | solution.py:639
  10.7 0.7 constant_dynamic-update-slice_fusion.4
  11.4 0.0 collective-permute-done.4.swapped.swap_ref
  11.5 0.6 collective-permute-start.5
  12.1 0.9 %collective-permute-start.6 = (f32[784,128]{1,0:T(8,128)S(1)}, f32[784,128]{1,0:T(8,128)S(1)}, u32[]{:S(2)}, u32[]{:S(2)}) collective-permute-start(f32[784,128]{1,0:T(8,128)S(1)} %get-tuple-element.37), channel_id=1, source_target_pairs={{0,6},{1,7},{2,0},{3,1},{4,2},{5,3},{6,4},{7,5},{8,14},{9,15},{10,... | collective-permute-start | bytes 1204232 | tf_op jit(solution)/shard_map/ppermute | solution.py:669
  13.0 1.5 %collective-permute-start.7 = (f32[784,128]{1,0:T(8,128)S(1)}, f32[784,128]{1,0:T(8,128)S(1)}, u32[]{:S(2)}, u32[]{:S(2)}) collective-permute-start(f32[784,128]{1,0:T(8,128)S(1)} %get-tuple-element.38), channel_id=1, source_target_pairs={{0,4},{1,5},{2,6},{3,7},{4,0},{5,1},{6,2},{7,3},{8,12},{9,13},{10,... | collective-permute-start | bytes 1204232 | tf_op jit(solution)/shard_map/ppermute | solution.py:669
  14.5 0.0 collective-permute-done.south_ref
  14.5 2.6 %collective-permute-done.1.north_ref = f32[288,128]{1,0:T(8,128)S(1)} collective-permute-done((f32[288,128]{1,0:T(8,128)S(1)}, f32[288,128]{1,0:T(8,128)S(1)}, u32[]{:S(2)}, u32[]{:S(2)}) %collective-permute-start.1) | collective-permute-done | bytes 147488 | tf_op jit(solution)/shard_map/ppermute | solution.py:639
  17.1 1.8 %widen.1 = (f32[4368,128]{1,0:T(8,128)S(1)}, f32[168,128]{1,0:T(8,128)S(1)}, f32[168,128]{1,0:T(8,128)S(1)}) custom-call(f32[3,48,24,128]{3,2,1,0:T(8,128)} %coef_ref.3, f32[288,128]{1,0:T(8,128)S(1)} %collective-permute-done.south_ref, f32[288,128]{1,0:T(8,128)S(1)} %collective-permute-done.1.north_ref), custom_call_target="tpu_custom_call" | custom-call | tf_op jit(solution)/shard_map/widen/pallas_call | solution.py:376
  18.9 1.1 %collective-permute-start.2 = (f32[168,128]{1,0:T(8,128)S(1)}, f32[168,128]{1,0:T(8,128)S(1)}, u32[]{:S(2)}, u32[]{:S(2)}) collective-permute-start(f32[168,128]{1,0:T(8,128)S(1)} %get-tuple-element.30), channel_id=1, source_target_pairs={{0,8},{8,16},{16,24},{24,0},{1,9},{9,17},{17,25},{25,1},{2,10},{10... | collective-permute-start | bytes 258056 | tf_op jit(solution)/shard_map/ppermute | solution.py:639
  20.0 1.3 %collective-permute-start.3 = (f32[168,128]{1,0:T(8,128)S(1)}, f32[168,128]{1,0:T(8,128)S(1)}, u32[]{:S(2)}, u32[]{:S(2)}) collective-permute-start(f32[168,128]{1,0:T(8,128)S(1)} %get-tuple-element.31), channel_id=1, source_target_pairs={{8,0},{16,8},{24,16},{0,24},{9,1},{17,9},{25,17},{1,25},{10,2},{18... | collective-permute-start | bytes 258056 | tf_op jit(solution)/shard_map/ppermute | solution.py:639
  21.4 2.7 %collective-permute-done.2.west = f32[168,128]{1,0:T(8,128)S(1)} collective-permute-done((f32[168,128]{1,0:T(8,128)S(1)}, f32[168,128]{1,0:T(8,128)S(1)}, u32[]{:S(2)}, u32[]{:S(2)}) %collective-permute-start.2) | collective-permute-done | bytes 86048 | tf_op jit(solution)/shard_map/ppermute | solution.py:639
  24.1 1.5 %collective-permute-done.3.east = f32[168,128]{1,0:T(8,128)S(1)} collective-permute-done((f32[168,128]{1,0:T(8,128)S(1)}, f32[168,128]{1,0:T(8,128)S(1)}, u32[]{:S(2)}, u32[]{:S(2)}) %collective-permute-start.3) | collective-permute-done | bytes 86048 | tf_op jit(solution)/shard_map/ppermute | solution.py:639
  25.6 4.3 %combine.1.rest_2_.coef_ref = f32[9128,128]{1,0:T(8,128)S(1)} custom-call(f32[4368,128]{1,0:T(8,128)S(1)} %get-tuple-element.29.ring_ref, f32[168,128]{1,0:T(8,128)S(1)} %collective-permute-done.2.west, f32[168,128]{1,0:T(8,128)S(1)} %collective-permute-done.3.east), custom_call_target="tpu_custom_call" | custom-call | tf_op jit(solution)/shard_map/combine/pallas_call | solution.py:434
  29.9 3.6 %scatter_own.1.rest_1_ = f32[7280,128]{1,0:T(8,128)S(1)} custom-call(s32[1,2560]{1,0:T(1,128)S(1)} %constant_dynamic-update-slice_fusion.table_ref, f32[5760,128]{1,0:T(8,128)} %bitcast.24, f32[392,128]{1,0:T(8,128)S(1)} %get-tuple-element.39.own_ref, f32[1568,128]{1,0:T(8,128)S(1)} %collective-permute-done.4.swapped.swap_ref), custom_call_target="tpu_custom_call" | custom-call | tf_op jit(solution)/shard_map/scatter_own/pallas_call | solution.py:270
  33.5 13.8 %collective-permute-done.7.rest_0_ = f32[784,128]{1,0:T(8,128)S(1)} collective-permute-done((f32[784,128]{1,0:T(8,128)S(1)}, f32[784,128]{1,0:T(8,128)S(1)}, u32[]{:S(2)}, u32[]{:S(2)}) %collective-permute-start.7) | collective-permute-done | bytes 401440 | tf_op jit(solution)/shard_map/ppermute | solution.py:669
  47.3 2.0 %scatter_more.1.rest_2_ = f32[7280,128]{1,0:T(8,128)S(1)} custom-call(s32[1,2560]{1,0:T(1,128)S(1)} %constant_dynamic-update-slice_fusion.table_ref, f32[784,128]{1,0:T(8,128)S(1)} %collective-permute-done.7.rest_0_, f32[7280,128]{1,0:T(8,128)S(1)} %scatter_own.1.rest_1_, f32[9128,128]{1,0:T(8,128)S(1)} %combine.1.rest_2_.coef_ref), custom_call_target="tpu_custom_call", output_to_operand_aliasing={{}: (2, {})} | custom-call | tf_op jit(solution)/shard_map/scatter_more/pallas_call | solution.py:325
  49.3 0.0 collective-permute-done.5.rest_0_
  49.3 3.3 %scatter_last.1 = (f32[7280,128]{1,0:T(8,128)S(1)}, f32[480,128]{1,0:T(8,128)S(1)}, f32[480,128]{1,0:T(8,128)S(1)}) custom-call(s32[1,2560]{1,0:T(1,128)S(1)} %constant_dynamic-update-slice_fusion.table_ref, f32[784,128]{1,0:T(8,128)S(1)} %collective-permute-done.5.rest_0_, ...), custom_call_target="tpu_custom_call", output_to_operand_aliasing={{0}: (3, {})} | custom-call | tf_op jit(solution)/shard_map/scatter_last/pallas_call | solution.py:325
  52.6 6.8 %collective-permute-start.8 = (f32[480,128]{1,0:T(8,128)S(1)}, f32[480,128]{1,0:T(8,128)S(1)}, u32[]{:S(2)}, u32[]{:S(2)}) collective-permute-start(f32[480,128]{1,0:T(8,128)S(1)} %get-tuple-element.41), channel_id=1, source_target_pairs={{0,1},{1,2},{2,3},{3,4},{4,5},{5,6},{6,7},{8,9},{9,10},{10,11},{11... | collective-permute-start | bytes 737288 | tf_op jit(solution)/shard_map/ppermute | solution.py:639
  59.4 1.9 %collective-permute-start.9 = (f32[480,128]{1,0:T(8,128)S(1)}, f32[480,128]{1,0:T(8,128)S(1)}, u32[]{:S(2)}, u32[]{:S(2)}) collective-permute-start(f32[480,128]{1,0:T(8,128)S(1)} %get-tuple-element.42), channel_id=1, source_target_pairs={{1,0},{2,1},{3,2},{4,3},{5,4},{6,5},{7,6},{9,8},{10,9},{11,10},{12... | collective-permute-start | bytes 737288 | tf_op jit(solution)/shard_map/ppermute | solution.py:639
  61.3 1.2 %collective-permute-done.8.south = f32[480,128]{1,0:T(8,128)S(1)} collective-permute-done((f32[480,128]{1,0:T(8,128)S(1)}, f32[480,128]{1,0:T(8,128)S(1)}, u32[]{:S(2)}, u32[]{:S(2)}) %collective-permute-start.8) | collective-permute-done | bytes 245792 | tf_op jit(solution)/shard_map/ppermute | solution.py:639
  62.5 6.7 %collective-permute-done.9.north = f32[480,128]{1,0:T(8,128)S(1)} collective-permute-done((f32[480,128]{1,0:T(8,128)S(1)}, f32[480,128]{1,0:T(8,128)S(1)}, u32[]{:S(2)}, u32[]{:S(2)}) %collective-permute-start.9) | collective-permute-done | bytes 245792 | tf_op jit(solution)/shard_map/ppermute | solution.py:639
  69.2 0.3 insert.1
  69.6 0.1 collective-permute-start.10
  69.7 2.4 %collective-permute-start.11 = (f32[280,128]{1,0:T(8,128)S(1)}, f32[280,128]{1,0:T(8,128)S(1)}, u32[]{:S(2)}, u32[]{:S(2)}) collective-permute-start(f32[280,128]{1,0:T(8,128)S(1)} %get-tuple-element.46), channel_id=1, source_target_pairs={{8,0},{16,8},{24,16},{0,24},{9,1},{17,9},{25,17},{1,25},{10,2},{18... | collective-permute-start | bytes 430088 | tf_op jit(solution)/shard_map/ppermute | solution.py:639
  72.0 11.0 %inner.1 = (f32[6520,128]{1,0:T(8,128)S(1)}, f32[5760,128]{1,0:T(8,128)}) custom-call(f32[9128,128]{1,0:T(8,128)S(1)} %combine.1.rest_2_.coef_ref, f32[7280,128]{1,0:T(8,128)S(1)} %get-tuple-element.43.state.state_in), custom_call_target="tpu_custom_call" | custom-call | tf_op jit(solution)/shard_map/inner/pallas_call | solution.py:555
  83.0 0.0 collective-permute-done.10.west
  83.0 1.7 %outer.1 = (f32[7280,128]{1,0:T(8,128)S(1)}, f32[6520,128]{1,0:T(8,128)S(1)}, f32[5760,128]{1,0:T(8,128)}) custom-call(f32[9128,128]{1,0:T(8,128)S(1)} %combine.1.rest_2_.coef_ref, f32[7280,128]{1,0:T(8,128)S(1)} %get-tuple-element.43.state.state_in, ...), custom_call_target="tpu_custom_call", output_to_operand_aliasing={{0}: (1, {}), {1}: (2, {}), {2}: (5, {})} | custom-call | tf_op jit(solution)/shard_map/outer/pallas_call | solution.py:617
  (7 shorter events, 0.1 us)
Async XLA Ops:
  4.7 6.7 %collective-permute-start.4 = (f32[1568,128]{1,0:T(8,128)S(1)}, f32[1568,128]{1,0:T(8,128)S(1)}, u32[]{:S(2)}, u32[]{:S(2)}) collective-permute-start(f32[1568,128]{1,0:T(8,128)S(1)} %get-tuple-element.32), channel_id=1, source_target_pairs={{0,1},{1,0},{2,3},{3,2},{4,5},{5,4},{6,7},{7,6},{8,9},{9,8},{10,11... | collective-permute-start | bytes 2408456 | tf_op jit(solution)/shard_map/ppermute | solution.py:664
  5.2 9.3 %collective-permute-start = (f32[288,128]{1,0:T(8,128)S(1)}, f32[288,128]{1,0:T(8,128)S(1)}, u32[]{:S(2)}, u32[]{:S(2)}) collective-permute-start(f32[288,128]{1,0:T(8,128)S(1)} %get-tuple-element.27), channel_id=1, source_target_pairs={{0,1},{1,2},{2,3},{3,4},{4,5},{5,6},{6,7},{8,9},{9,10},{10,11},{11... | collective-permute-start | bytes 442376 | tf_op jit(solution)/shard_map/ppermute | solution.py:639
  8.7 8.3 %collective-permute-start.1 = (f32[288,128]{1,0:T(8,128)S(1)}, f32[288,128]{1,0:T(8,128)S(1)}, u32[]{:S(2)}, u32[]{:S(2)}) collective-permute-start(f32[288,128]{1,0:T(8,128)S(1)} %get-tuple-element.28), channel_id=1, source_target_pairs={{1,0},{2,1},{3,2},{4,3},{5,4},{6,5},{7,6},{9,8},{10,9},{11,10},{12... | collective-permute-start | bytes 442376 | tf_op jit(solution)/shard_map/ppermute | solution.py:639
  11.5 37.8 %collective-permute-start.5 = (f32[784,128]{1,0:T(8,128)S(1)}, f32[784,128]{1,0:T(8,128)S(1)}, u32[]{:S(2)}, u32[]{:S(2)}) collective-permute-start(f32[784,128]{1,0:T(8,128)S(1)} %get-tuple-element.36), channel_id=1, source_target_pairs={{0,2},{1,3},{2,4},{3,5},{4,6},{5,7},{6,0},{7,1},{8,10},{9,11},{10,... | collective-permute-start | bytes 1204232 | tf_op jit(solution)/shard_map/ppermute | solution.py:669
  12.1 37.2 %collective-permute-start.6 = (f32[784,128]{1,0:T(8,128)S(1)}, f32[784,128]{1,0:T(8,128)S(1)}, u32[]{:S(2)}, u32[]{:S(2)}) collective-permute-start(f32[784,128]{1,0:T(8,128)S(1)} %get-tuple-element.37), channel_id=1, source_target_pairs={{0,6},{1,7},{2,0},{3,1},{4,2},{5,3},{6,4},{7,5},{8,14},{9,15},{10,... | collective-permute-start | bytes 1204232 | tf_op jit(solution)/shard_map/ppermute | solution.py:669
  13.0 34.3 %collective-permute-start.7 = (f32[784,128]{1,0:T(8,128)S(1)}, f32[784,128]{1,0:T(8,128)S(1)}, u32[]{:S(2)}, u32[]{:S(2)}) collective-permute-start(f32[784,128]{1,0:T(8,128)S(1)} %get-tuple-element.38), channel_id=1, source_target_pairs={{0,4},{1,5},{2,6},{3,7},{4,0},{5,1},{6,2},{7,3},{8,12},{9,13},{10,... | collective-permute-start | bytes 1204232 | tf_op jit(solution)/shard_map/ppermute | solution.py:669
  18.9 5.1 %collective-permute-start.2 = (f32[168,128]{1,0:T(8,128)S(1)}, f32[168,128]{1,0:T(8,128)S(1)}, u32[]{:S(2)}, u32[]{:S(2)}) collective-permute-start(f32[168,128]{1,0:T(8,128)S(1)} %get-tuple-element.30), channel_id=1, source_target_pairs={{0,8},{8,16},{16,24},{24,0},{1,9},{9,17},{17,25},{25,1},{2,10},{10... | collective-permute-start | bytes 258056 | tf_op jit(solution)/shard_map/ppermute | solution.py:639
  20.0 5.6 %collective-permute-start.3 = (f32[168,128]{1,0:T(8,128)S(1)}, f32[168,128]{1,0:T(8,128)S(1)}, u32[]{:S(2)}, u32[]{:S(2)}) collective-permute-start(f32[168,128]{1,0:T(8,128)S(1)} %get-tuple-element.31), channel_id=1, source_target_pairs={{8,0},{16,8},{24,16},{0,24},{9,1},{17,9},{25,17},{1,25},{10,2},{18... | collective-permute-start | bytes 258056 | tf_op jit(solution)/shard_map/ppermute | solution.py:639
  52.6 9.9 %collective-permute-start.8 = (f32[480,128]{1,0:T(8,128)S(1)}, f32[480,128]{1,0:T(8,128)S(1)}, u32[]{:S(2)}, u32[]{:S(2)}) collective-permute-start(f32[480,128]{1,0:T(8,128)S(1)} %get-tuple-element.41), channel_id=1, source_target_pairs={{0,1},{1,2},{2,3},{3,4},{4,5},{5,6},{6,7},{8,9},{9,10},{10,11},{11... | collective-permute-start | bytes 737288 | tf_op jit(solution)/shard_map/ppermute | solution.py:639
  59.4 9.8 %collective-permute-start.9 = (f32[480,128]{1,0:T(8,128)S(1)}, f32[480,128]{1,0:T(8,128)S(1)}, u32[]{:S(2)}, u32[]{:S(2)}) collective-permute-start(f32[480,128]{1,0:T(8,128)S(1)} %get-tuple-element.42), channel_id=1, source_target_pairs={{1,0},{2,1},{3,2},{4,3},{5,4},{6,5},{7,6},{9,8},{10,9},{11,10},{12... | collective-permute-start | bytes 737288 | tf_op jit(solution)/shard_map/ppermute | solution.py:639
  69.6 13.4 %collective-permute-start.10 = (f32[280,128]{1,0:T(8,128)S(1)}, f32[280,128]{1,0:T(8,128)S(1)}, u32[]{:S(2)}, u32[]{:S(2)}) collective-permute-start(f32[280,128]{1,0:T(8,128)S(1)} %get-tuple-element.45), channel_id=1, source_target_pairs={{0,8},{8,16},{16,24},{24,0},{1,9},{9,17},{17,25},{25,1},{2,10},{10... | collective-permute-start | bytes 430088 | tf_op jit(solution)/shard_map/ppermute | solution.py:639
  69.7 13.4 %collective-permute-start.11 = (f32[280,128]{1,0:T(8,128)S(1)}, f32[280,128]{1,0:T(8,128)S(1)}, u32[]{:S(2)}, u32[]{:S(2)}) collective-permute-start(f32[280,128]{1,0:T(8,128)S(1)} %get-tuple-element.46), channel_id=1, source_target_pairs={{8,0},{16,8},{24,16},{0,24},{9,1},{17,9},{25,17},{1,25},{10,2},{18... | collective-permute-start | bytes 430088 | tf_op jit(solution)/shard_map/ppermute | solution.py:639

commit v2 on v1

--- a/solution.py
+++ b/solution.py
@@ -42,14 +42,34 @@
     wait_all(copies)
 
 
+def pairs_of(axis, periodic):
+    count = lax.axis_size(axis)
+    near = [(i, i ^ 1) for i in range(count)]
+    across = []
+    for i in range(1, count, 2):
+        if periodic or i + 1 < count:
+            across += [(i, (i + 1) % count), ((i + 1) % count, i)]
+    return near, across
+
+
+def swap_sides(near, across, axis, periodic):
+    near_pairs, across_pairs = pairs_of(axis, periodic)
+    return lax.ppermute(near, axis, near_pairs), lax.ppermute(across, axis, across_pairs)
+
+
+def near_side(low, high, axis="lat"):
+    odd = (lax.axis_index(axis) & 1) == 1
+    return jnp.where(odd, low, high), jnp.where(odd, high, low)
+
+
 def pack_kernel(
     n, cap, stations, count_ref, band_ref, station_ref, var_ref, dep_ref, coef_ref, *rest
 ):
     half = n // 2
     own, swap = rest[:2]
     through = rest[2 : half + 1]
-    south, north = rest[half + 1 : half + 3]
-    (dep, band, station, var, low, high, buf, pos_v, pos_s, sem) = rest[half + 3 :]
+    near, across = rest[half + 1 : half + 3]
+    (dep, band, station, var, edge, buf, pos_v, pos_s, sem) = rest[half + 3 :]
     me = lax.axis_index("lat")
     rows, lanes = band.shape
     lat_cells = coef_ref.shape[2]
@@ -61,8 +81,8 @@
                 (station_ref, station),
                 (var_ref, var),
                 (dep_ref, dep),
-                (coef_ref.at[:, :, pl.ds(0, 8)], low),
-                (coef_ref.at[:, :, pl.ds(lat_cells - 8, 8)], high),
+                (coef_ref.at[:, :, pl.ds(0, 8)], edge.at[0]),
+                (coef_ref.at[:, :, pl.ds(lat_cells - 8, 8)], edge.at[1]),
             )
         )
     ]
@@ -131,12 +151,13 @@
             to[pl.ds(at + cap + j, 1), :] = codes[s : s + 1, j * lanes : (j + 1) * lanes]
         to[pl.ds(at + cap + HEADER - 1, 1), :] = counts[(s + 1) * rows - 1 : (s + 1) * rows]
     wait_all(loads[3:])
-    fields, lons = low.shape[:2]
+    fields, lons = edge.shape[1:3]
+    odd = me & 1
 
     def strip(i, carry):
         for f in range(fields):
-            north[pl.ds((f * lons + i) * 2, 2), :] = high[f, i, 6:8]
-            south[pl.ds((f * lons + i) * 2, 2), :] = low[f, i, 0:2]
+            near[pl.ds((f * lons + i) * 2, 2), :] = edge[1 - odd, f, i, pl.ds(6 - 6 * odd, 2), :]
+            across[pl.ds((f * lons + i) * 2, 2), :] = edge[odd, f, i, pl.ds(6 * odd, 2), :]
         return carry
 
     lax.fori_loop(0, lons, strip, 0)
@@ -174,8 +195,7 @@
             V((rows, LANES), jnp.int32),
             V((rows, LANES), jnp.int32),
             V((rows, LANES), jnp.int32),
-            V((fields, lons, 8, LANES), jnp.float32),
-            V((fields, lons, 8, LANES), jnp.float32),
+            V((2, fields, lons, 8, LANES), jnp.float32),
             V((n * STRIDE + HEADER + STRIDE, LANES), jnp.float32),
             V((rows, LANES), jnp.int32),
             pltpu.SMEM((rows, LANES), jnp.int32),
@@ -186,23 +206,24 @@
     )(count, *(in_hbm(array) for array in (band, station, var, dep, coef)))
 
 
-def relay_kernel(k, size, swapped, *rest):
-    for j, to in enumerate(rest[k:]):
-        to[pl.ds(size, size), :] = swapped[pl.ds((j + 1) * size, size), :]
-
-
-def relay(swapped, through, size):
-    k = len(through)
-    vm = pl.BlockSpec(memory_space=V)
-    return pl.pallas_call(
-        functools.partial(relay_kernel, k, size),
-        out_shape=tuple(V(array.shape, jnp.float32) for array in through),
-        in_specs=[vm] * (k + 1),
+def relay_kernel(shifts, size, swapped, *rest):
+    for s, to in zip(shifts, rest[len(rest) - len(shifts) :]):
+        to[pl.ds(size, size), :] = swapped[pl.ds(s * size, size), :]
+
+
+def relay(swapped, through, shifts, size, after=()):
+    k = len(shifts)
+    vm = pl.BlockSpec(memory_space=V)
+    picked = [through[s - 1] for s in shifts]
+    return pl.pallas_call(
+        functools.partial(relay_kernel, shifts, size),
+        out_shape=tuple(V(array.shape, jnp.float32) for array in picked),
+        in_specs=[vm] * (k + 1 + len(after)),
         out_specs=(vm,) * k,
         input_output_aliases={j + 1: j for j in range(k)},
         compiler_params=params(),
         name="relay",
-    )(in_vmem(swapped), *(in_vmem(array) for array in through))
+    )(in_vmem(swapped), *(in_vmem(array) for array in (*picked, *after)))
 
 
 def open_header(packet, base, cap, view, header, sem):
@@ -300,17 +321,18 @@
         scatter_packet(table_ref, *packets[j], headers[j], state)
     if not last:
         return
-    south, north = outs[1:]
+    near, across = outs[1:]
     span = lats + 4
     ring = (lons + 4) * span
     nv = state.shape[0] // ring
+    near_row, across_row = near_side(2, lats)
 
     def strip(i, carry):
         for v in range(nv):
             at = v * ring + (i + 2) * span
             to = (v * lons + i) * 2
-            south[pl.ds(to, 2), :] = state[pl.ds(at + 2, 2), :]
-            north[pl.ds(to, 2), :] = state[pl.ds(at + lats, 2), :]
+            near[pl.ds(to, 2), :] = state[pl.ds(at + near_row, 2), :]
+            across[pl.ds(to, 2), :] = state[pl.ds(at + across_row, 2), :]
         return carry
 
     lax.fori_loop(0, lons, strip, 0)
@@ -341,13 +363,12 @@
     )
 
 
-def widen_kernel(coef_ref, south_ref, north_ref, ring_out, west, east, own, sem):
+def widen_kernel(coef_ref, near_ref, across_ref, after, ring_out, near_lon, across_lon, own, sem):
     fields, lons, lats, _ = coef_ref.shape
     span = lats + 4
     ring = (lons + 4) * span
-    me = lax.axis_index("lat")
-    has_south = (me > 0).astype(jnp.float32)
-    has_north = (me < lax.axis_size("lat") - 1).astype(jnp.float32)
+    near_row, across_row = near_side(0, lats + 2)
+    near_at, across_at = near_side(2 * span, lons * span, "lon")
     run([pltpu.make_async_copy(coef_ref, own, sem)])
 
     def fill(i, carry):
@@ -356,19 +377,27 @@
             at = (f * lons + i) * 2
             for r in range(0, lats, 8):
                 ring_out[pl.ds(to + 2 + r, 8), :] = own[f, i, r : r + 8]
-            ring_out[pl.ds(to, 2), :] = south_ref[pl.ds(at, 2), :] * has_south
-            ring_out[pl.ds(to + lats + 2, 2), :] = north_ref[pl.ds(at, 2), :] * has_north
+            ring_out[pl.ds(to + near_row, 2), :] = near_ref[pl.ds(at, 2), :]
+            ring_out[pl.ds(to + across_row, 2), :] = across_ref[pl.ds(at, 2), :]
         return carry
 
     lax.fori_loop(0, lons, fill, 0)
-    for f in range(fields):
-        west[pl.ds(f * 2 * span, 2 * span), :] = ring_out[pl.ds(f * ring + 2 * span, 2 * span), :]
-        east[pl.ds(f * 2 * span, 2 * span), :] = ring_out[
-            pl.ds(f * ring + lons * span, 2 * span), :
-        ]
-
-
-def widen(coef, south, north):
+    take_lons(ring_out, near_lon, across_lon, fields, ring, 2 * span, near_at, across_at)
+
+
+def take_lons(ring_ref, near, across, count, ring, size, near_at, across_at):
+    for f in range(count):
+        near[pl.ds(f * size, size), :] = ring_ref[pl.ds(f * ring + near_at, size), :]
+        across[pl.ds(f * size, size), :] = ring_ref[pl.ds(f * ring + across_at, size), :]
+
+
+def put_lons(ring_ref, near, across, count, ring, size, near_at, across_at):
+    for f in range(count):
+        ring_ref[pl.ds(f * ring + near_at, size), :] = near[pl.ds(f * size, size), :]
+        ring_ref[pl.ds(f * ring + across_at, size), :] = across[pl.ds(f * size, size), :]
+
+
+def widen(coef, near, across, after):
     fields, lons, lats, _ = coef.shape
     span = lats + 4
     vm = pl.BlockSpec(memory_space=V)
@@ -376,26 +405,23 @@
     return pl.pallas_call(
         widen_kernel,
         out_shape=(V((fields * (lons + 4) * span, LANES), jnp.float32), edge, edge),
-        in_specs=[pl.BlockSpec(memory_space=pltpu.HBM), vm, vm],
+        in_specs=[pl.BlockSpec(memory_space=pltpu.HBM), vm, vm, vm],
         out_specs=(vm, vm, vm),
         scratch_shapes=[V(coef.shape, jnp.float32), pltpu.SemaphoreType.DMA],
         compiler_params=params(),
         name="widen",
-    )(in_hbm(coef), in_vmem(south), in_vmem(north))
-
-
-def combine_kernel(lons, lats, ring_ref, west, east, out_ref, field):
+    )(in_hbm(coef), in_vmem(near), in_vmem(across), in_vmem(after))
+
+
+def combine_kernel(lons, lats, ring_ref, near, across, out_ref, field):
     me = lax.axis_index("lat")
     total = lats * lax.axis_size("lat")
     span, rim = lats + 4, lats + 2
     ring = (lons + 4) * span
     size = rim_rows(lons, lats)
     field[...] = ring_ref[...]
-    for f in range(field.shape[0] // ring):
-        field[pl.ds(f * ring, 2 * span), :] = west[pl.ds(f * 2 * span, 2 * span), :]
-        field[pl.ds(f * ring + (lons + 2) * span, 2 * span), :] = east[
-            pl.ds(f * 2 * span, 2 * span), :
-        ]
+    ends = near_side(0, (lons + 2) * span, "lon")
+    put_lons(field, near, across, field.shape[0] // ring, ring, 2 * span, *ends)
     lev = lax.broadcasted_iota(jnp.int32, (8, LANES), 1)
     row = lax.broadcasted_iota(jnp.int32, (8, LANES), 0)
 
@@ -429,7 +455,7 @@
     lax.fori_loop(0, lons + 2, one, 0)
 
 
-def combine(ring, west, east, lons, lats):
+def combine(ring, near, across, lons, lats):
     vm = pl.BlockSpec(memory_space=V)
     return pl.pallas_call(
         functools.partial(combine_kernel, lons, lats),
@@ -439,7 +465,7 @@
         scratch_shapes=[V(ring.shape, jnp.float32)],
         compiler_params=params(),
         name="combine",
-    )(in_vmem(ring), in_vmem(west), in_vmem(east))
+    )(in_vmem(ring), in_vmem(near), in_vmem(across))
 
 
 def rim_rows(lons, lats):
@@ -453,25 +479,41 @@
     return starts
 
 
-def weighted(factors, source, at, east):
-    centre = source[pl.ds(at, 8), :]
-    total = factors[0] * centre + factors[1] * source[pl.ds(at + east, 8), :]
-    other = factors[2] * source[pl.ds(at - east, 8), :] + factors[3] * source[pl.ds(at + 1, 8), :]
-    third = factors[4] * source[pl.ds(at - 1, 8), :] + factors[5] * pltpu.roll(
-        centre, LANES - 1, 1
-    )
+def weighted(factors, source, at, east, rows=None):
+    rows = rows or (lambda start: pl.ds(start, 8))
+    centre = source[rows(at), :]
+    total = factors[0] * centre + factors[1] * source[rows(at + east), :]
+    other = factors[2] * source[rows(at - east), :] + factors[3] * source[rows(at + 1), :]
+    third = factors[4] * source[rows(at - 1), :] + factors[5] * pltpu.roll(centre, LANES - 1, 1)
     return (total + other) + (third + factors[6] * pltpu.roll(centre, 1, 1))
 
 
-def first_step(coef_ref, state, mid, nv, lons, lats, i):
+def first_step(coef_ref, state, mid, nv, lons, lats, i, starts):
     span, rim = lats + 4, lats + 2
     ring, size = (lons + 4) * span, rim_rows(lons, lats)
-    for r in chunks(rim):
+    for r in starts:
         factors = [coef_ref[pl.ds(k * size + i * rim + r, 8), :] for k in range(7)]
         for v in range(nv):
             mid[pl.ds(v * size + i * rim + r, 8), :] = weighted(
                 factors, state, v * ring + (i + 1) * span + r + 1, span
             )
+
+
+def first_step_along(coef_ref, state, mid, nv, lons, lats, i, r):
+    span, rim = lats + 4, lats + 2
+    ring, size = (lons + 4) * span, rim_rows(lons, lats)
+
+    def rim_at(start):
+        return pl.ds(start, 8, stride=rim)
+
+    def ring_at(start):
+        return pl.ds(start, 8, stride=span)
+
+    factors = [coef_ref[rim_at(k * size + i * rim + r), :] for k in range(7)]
+    for v in range(nv):
+        mid[rim_at(v * size + i * rim + r), :] = weighted(
+            factors, state, v * ring + (i + 1) * span + r + 1, span, ring_at
+        )
 
 
 def second_step(coef_ref, mid, out, nv, lons, lats, i, place):
@@ -486,26 +528,27 @@
             )
 
 
-def insert_kernel(lons, lats, state_in, south, north, state, west, east):
+def insert_kernel(lons, lats, state_in, near, across, state, near_lon, across_lon):
     span = lats + 4
     ring = (lons + 4) * span
     nv = state.shape[0] // ring
+
+    near_row, across_row = near_side(0, lats + 2)
 
     def strip(i, carry):
         for v in range(nv):
             at = v * ring + (i + 2) * span
             frm = (v * lons + i) * 2
-            state[pl.ds(at, 2), :] = south[pl.ds(frm, 2), :]
-            state[pl.ds(at + lats + 2, 2), :] = north[pl.ds(frm, 2), :]
+            state[pl.ds(at + near_row, 2), :] = near[pl.ds(frm, 2), :]
+            state[pl.ds(at + across_row, 2), :] = across[pl.ds(frm, 2), :]
         return carry
 
     lax.fori_loop(0, lons, strip, 0)
-    for v in range(nv):
-        west[pl.ds(v * 2 * span, 2 * span), :] = state[pl.ds(v * ring + 2 * span, 2 * span), :]
-        east[pl.ds(v * 2 * span, 2 * span), :] = state[pl.ds(v * ring + lons * span, 2 * span), :]
-
-
-def insert(state, south, north, shape):
+    ends = near_side(2 * span, lons * span, "lon")
+    take_lons(state, near_lon, across_lon, nv, ring, 2 * span, *ends)
+
+
+def insert(state, near, across, shape):
     nv, lons, lats = shape
     vm = pl.BlockSpec(memory_space=V)
     edge = V((nv * 2 * (lats + 4), LANES), jnp.float32)
@@ -517,18 +560,43 @@
         input_output_aliases={0: 0},
         compiler_params=params(),
         name="insert",
-    )(in_vmem(state), in_vmem(south), in_vmem(north))
-
-
-def inner_kernel(lons, lats, coef_ref, state, mid, out_ref, out, sem):
+    )(in_vmem(state), in_vmem(near), in_vmem(across))
+
+
+def early_kernel(nv, lons, lats, coef_ref, state, mid):
+    starts = [r + 2 for r in chunks(lats - 2)]
+
+    def first(i, carry):
+        first_step(coef_ref, state, mid, nv, lons, lats, i, starts)
+        return carry
+
+    lax.fori_loop(2, lons, first, 0)
+
+
+def early(coef, state, shape):
+    nv, lons, lats = shape
+    vm = pl.BlockSpec(memory_space=V)
+    return pl.pallas_call(
+        functools.partial(early_kernel, nv, lons, lats),
+        out_shape=V((nv * rim_rows(lons, lats), LANES), jnp.float32),
+        in_specs=[vm, vm],
+        out_specs=vm,
+        compiler_params=params(),
+        name="early",
+    )(in_vmem(coef), in_vmem(state))
+
+
+def inner_kernel(lons, lats, coef_ref, state, mid_in, mid, out_ref, out, sem):
     nv = out.shape[0] // (lons * lats)
     cells = lons * lats
-
-    def first(i, carry):
-        first_step(coef_ref, state, mid, nv, lons, lats, i)
-        return carry
-
-    lax.fori_loop(2, lons, first, 0)
+    for r in (0, 1, lats, lats + 1):
+
+        def first(k, carry, r=r):
+            i = jnp.minimum(2 + 8 * k, lons - 8)
+            first_step_along(coef_ref, state, mid, nv, lons, lats, i, r)
+            return carry
+
+        lax.fori_loop(0, -(-(lons - 2) // 8), first, 0)
 
     def second(i, carry):
         second_step(
@@ -549,42 +617,40 @@
     wait_all(copies)
 
 
-def inner(coef, state, shape):
+def inner(coef, state, mid, shape):
     nv, lons, lats = shape
     vm = pl.BlockSpec(memory_space=V)
     return pl.pallas_call(
         functools.partial(inner_kernel, lons, lats),
         out_shape=(
-            V((nv * rim_rows(lons, lats), LANES), jnp.float32),
+            V(mid.shape, jnp.float32),
             jax.ShapeDtypeStruct((nv * lons * lats, LANES), jnp.float32),
         ),
-        in_specs=[vm, vm],
+        in_specs=[vm, vm, vm],
         out_specs=(vm, pl.BlockSpec(memory_space=pltpu.HBM)),
+        input_output_aliases={2: 0},
         scratch_shapes=[
             V((nv * lons * lats, LANES), jnp.float32),
             pltpu.SemaphoreType.DMA((4 * nv,)),
         ],
         compiler_params=params(),
         name="inner",
-    )(in_vmem(coef), in_vmem(state))
+    )(in_vmem(coef), in_vmem(state), in_vmem(mid))
 
 
 def outer_kernel(
-    lons, lats, coef_ref, state_in, mid_in, west, east, out_in, state, mid, out_ref, out, sem
+    lons, lats, coef_ref, state_in, mid_in, near, across, out_in, state, mid, out_ref, out, sem
 ):
     span = lats + 4
     ring = (lons + 4) * span
     nv = state.shape[0] // ring
     cells = lons * lats
-    for v in range(nv):
-        state[pl.ds(v * ring, 2 * span), :] = west[pl.ds(v * 2 * span, 2 * span), :]
-        state[pl.ds(v * ring + (lons + 2) * span, 2 * span), :] = east[
-            pl.ds(v * 2 * span, 2 * span), :
-        ]
+    ends = near_side(0, (lons + 2) * span, "lon")
+    put_lons(state, near, across, nv, ring, 2 * span, *ends)
 
     def first(k, carry):
         i = jnp.where(k < 2, k, lons - 2 + k)
-        first_step(coef_ref, state, mid, nv, lons, lats, i)
+        first_step(coef_ref, state, mid, nv, lons, lats, i, chunks(lats + 2))
         return carry
 
     lax.fori_loop(0, 4, first, 0)
@@ -610,7 +676,7 @@
     run(copies)
 
 
-def outer(coef, state, mid, west, east, out, shape):
+def outer(coef, state, mid, near, across, out, shape):
     nv, lons, lats = shape
     vm = pl.BlockSpec(memory_space=V)
     hbm = pl.BlockSpec(memory_space=pltpu.HBM)
@@ -627,16 +693,7 @@
         scratch_shapes=[V((nv * 4 * lats, LANES), jnp.float32), pltpu.SemaphoreType.DMA((2 * nv,))],
         compiler_params=params(),
         name="outer",
-    )(in_vmem(coef), in_vmem(state), in_vmem(mid), in_vmem(west), in_vmem(east), out)[2]
-
-
-def from_sides(low_part, high_part, axis, periodic):
-    count = lax.axis_size(axis)
-    forward = [(i, i + 1) for i in range(count - 1)]
-    if periodic:
-        forward.append((count - 1, 0))
-    backward = [(target, source) for source, target in forward]
-    return lax.ppermute(high_part, axis, forward), lax.ppermute(low_part, axis, backward)
+    )(in_vmem(coef), in_vmem(state), in_vmem(mid), in_vmem(near), in_vmem(across), out)[2]
 
 
 def body(
@@ -660,33 +717,41 @@
         departures.reshape(slots, levels),
         coefficients,
     )
-    through, (south, north) = rest[:-2], rest[-2:]
+    through, (near, across) = rest[:-2], rest[-2:]
     swapped = lax.ppermute(swap, "lat", [(i, i ^ 1) for i in range(n)])
-    south, north = from_sides(south, north, "lat", False)
-    through = relay(swapped, through, cap + HEADER)
+    near, across = swap_sides(near, across, "lat", False)
+    size = cap + HEADER
     order = sorted(range(1, n // 2), key=lambda s: abs(4 * s - n))
-    moved = [
-        lax.ppermute(through[s - 1], "lat", [(i, (i + 2 * s) % n) for i in range(n)])
-        for s in order
-    ]
     cell = station_cell.reshape(1, stations)
     span = lats + 4
     spot = (cell // lats + 2) * span + cell % lats + 2
     tile = (lons + 4) * span
     table = jnp.concatenate([spot + v * tile for v in range(nv)], axis=1)
+    def send(shifts, after):
+        return [
+            lax.ppermute(packet, "lat", [(i, (i + 2 * s) % n) for i in range(n)])
+            for s, packet in zip(shifts, relay(swapped, through, shifts, size, after))
+        ]
+
+    middle = 1 + (len(order) - 1) // 2
+    first = relay(swapped, through, order[:1], size)
+    moved = [lax.ppermute(first[0], "lat", [(i, (i + 2 * order[0]) % n) for i in range(n)])]
     state = scatter_first(
         table, adjoint_in.reshape(nv * lons * lats, levels), own, swapped, cap, shape
     )
-    ring, west, east = widen(coefficients, south, north)
-    west, east = from_sides(west, east, "lon", True)
-    coef = combine(ring, west, east, lons, lats)
-    state = scatter_more(table, state, moved[:1], cap, shape, False, (coef,))
-    state, south, north = scatter_more(table, state, moved[1:], cap, shape, True)
-    south, north = from_sides(south, north, "lat", False)
-    state, west, east = insert(state, south, north, shape)
-    west, east = from_sides(west, east, "lon", True)
-    mid, out = inner(coef, state, shape)
-    out = outer(coef, state, mid, west, east, out, shape)
+    second = send(order[1:middle], (state,))
+    ring, near, across = widen(coefficients, near, across, state)
+    third = send(order[middle:], (ring,))
+    near, across = swap_sides(near, across, "lon", True)
+    coef = combine(ring, near, across, lons, lats)
+    state = scatter_more(table, state, moved, cap, shape, False)
+    state, near, across = scatter_more(table, state, second + third, cap, shape, True, (coef,))
+    near, across = swap_sides(near, across, "lat", False)
+    mid = early(coef, state, shape)
+    state, near, across = insert(state, near, across, shape)
+    near, across = swap_sides(near, across, "lon", True)
+    mid, out = inner(coef, state, mid, shape)
+    out = outer(coef, state, mid, near, across, out, shape)
     return out.reshape(adjoint_in.shape)
 
 

time: 85.3 us -> 75.1 us (0.88)
  the two profiles are of different devices: /device:TPU:17 before, /device:TPU:1 now
where the time goes in v2:
time: 75.1 us; the launch traced here: 74.5 us
  Pallas kernels  33.6 us (45%)
  starting transfers between devices  21.1 us (28%)
  waiting for transfers between devices  18.2 us (24%)
  between operations  0.83 us (1%)
    ppermute x4, starting transfers between devices, swap_sides(): lax.ppermute(across, axis, across_pairs)  11.5 us
    pallas_call x1, Pallas kernels, inner(): pl.pallas_call(functools.partial(inner_kernel, lons, lats), out_shape=(V(...  7.63 us
    ppermute x1, waiting for transfers between devices, body(): lax.ppermute(first[0], 'lat', [(i, (i + 2 * order[0]) % n) for i in range...  6.66 us
    ppermute x2, waiting for transfers between devices, send(): lax.ppermute(packet, 'lat', [(i, (i + 2 * s) % n) for i in range(n)])  5.47 us
    pallas_call x2, Pallas kernels, scatter_more(): pl.pallas_call(functools.partial(more_kernel, k, lons, lats, cap, last),...  5.06 us
    pallas_call x1, Pallas kernels, early(): pl.pallas_call(functools.partial(early_kernel, nv, lons, lats), out_shape...  4.87 us
    pallas_call x1, Pallas kernels, combine(): pl.pallas_call(functools.partial(combine_kernel, lons, lats), out_shape=V...  4.32 us
    pallas_call x1, Pallas kernels, pack(): pl.pallas_call(functools.partial(pack_kernel, n, cap, stations), out_shap...  4.13 us
  transfers between devices with their start and end apart: 12, of which 5 were waited for; matrix products, arithmetic and copies ran while one was open for 1% of the time, Pallas kernels for 33%

profile of v2, /device:TPU:1, one launch (start us, length us, event | category | flops | bytes accessed | tf_op | source)
XLA Modules:
  0.0 74.5 jit_solution(10911991810388070196)
XLA Ops:
  0.7 4.1 %pack.1 = (f32[392,128]{1,0:T(8,128)S(1)}, f32[1568,128]{1,0:T(8,128)S(1)}, f32[784,128]{1,0:T(8,128)S(1)}, f32[784,128]{1,0:T(8,128)S(1)}, f32[784,128]{1,0:T(8...) custom-call(s32[1,1]{1,0:T(1,128)S(6)} %copy.33.count_ref, s32[8,128]{1,0:T(8,128)} %bitcast.26, ...), custom_call_target="tpu_custom_call" | custom-call | tf_op jit(solution)/shard_map/pack/pallas_call | solution.py:188
  4.8 0.1 collective-permute-start
  4.9 4.7 %collective-permute-start.1 = (f32[288,128]{1,0:T(8,128)S(1)}, f32[288,128]{1,0:T(8,128)S(1)}, u32[]{:S(2)}, u32[]{:S(2)}) collective-permute-start(f32[288,128]{1,0:T(8,128)S(1)} %get-tuple-element.25), channel_id=1, source_target_pairs={{1,2},{2,1},{3,4},{4,3},{5,6},{6,5},{9,10},{10,9},{11,12},{12,11},... | collective-permute-start | bytes 442376 | tf_op jit(solution)/shard_map/ppermute | solution.py:57
  9.5 0.1 collective-permute-start.2
  9.6 0.7 constant_dynamic-update-slice_fusion.4
  10.4 1.5 %collective-permute-done.2.swap_ref.swapped = f32[1568,128]{1,0:T(8,128)S(1)} collective-permute-done((f32[1568,128]{1,0:T(8,128)S(1)}, f32[1568,128]{1,0:T(8,128)S(1)}, u32[]{:S(2)}, u32[]{:S(2)}) %collective-permute-start.2) | collective-permute-done | bytes 802848 | tf_op jit(solution)/shard_map/ppermute | solution.py:721
  11.9 2.1 %collective-permute-start.7 = (f32[784,128]{1,0:T(8,128)S(1)}, f32[784,128]{1,0:T(8,128)S(1)}, u32[]{:S(2)}, u32[]{:S(2)}) collective-permute-start(f32[784,128]{1,0:T(8,128)S(1)} %relay.5), channel_id=1, source_target_pairs={{0,4},{1,5},{2,6},{3,7},{4,0},{5,1},{6,2},{7,3},{8,12},{9,13},{10,... | collective-permute-start | bytes 1204232 | tf_op jit(solution)/shard_map/ppermute | solution.py:738
  14.1 3.5 %scatter_own.1.after.rest_1_ = f32[7280,128]{1,0:T(8,128)S(1)} custom-call(s32[1,2560]{1,0:T(1,128)S(1)} %constant_dynamic-update-slice_fusion.table_ref, f32[5760,128]{1,0:T(8,128)} %bitcast.24, f32[392,128]{1,0:T(8,128)S(1)} %get-tuple-element.26.own_ref, f32[1568,128]{1,0:T(8,128)S(1)} %collective-permute-done.2.swap_ref.swapped), custom_call_target="tpu_custom_call" | custom-call | tf_op jit(solution)/shard_map/scatter_own/pallas_call | solution.py:291
  17.6 1.3 %collective-permute-start.5 = (f32[784,128]{1,0:T(8,128)S(1)}, f32[784,128]{1,0:T(8,128)S(1)}, u32[]{:S(2)}, u32[]{:S(2)}) collective-permute-start(f32[784,128]{1,0:T(8,128)S(1)} %relay.3), channel_id=1, source_target_pairs={{0,2},{1,3},{2,4},{3,5},{4,6},{5,7},{6,0},{7,1},{8,10},{9,11},{10,... | collective-permute-start | bytes 1204232 | tf_op jit(solution)/shard_map/ppermute | solution.py:732
  18.9 0.0 collective-permute-done.near_ref
  18.9 1.9 %widen.1 = (f32[4368,128]{1,0:T(8,128)S(1)}, f32[168,128]{1,0:T(8,128)S(1)}, f32[168,128]{1,0:T(8,128)S(1)}) custom-call(f32[3,48,24,128]{3,2,1,0:T(8,128)} %coef_ref.3, f32[288,128]{1,0:T(8,128)S(1)} %collective-permute-done.near_ref, f32[288,128]{1,0:T(8,128)S(1)} %collective-permute-done.1.across_ref, f32[7280,128]{1,0:T(8,128)S(1)} %scatter_own.1.after.rest_1_), custom_call_target="tpu_custom_call" | custom-call | tf_op jit(solution)/shard_map/widen/pallas_call | solution.py:405
  20.9 2.1 %collective-permute-start.6 = (f32[784,128]{1,0:T(8,128)S(1)}, f32[784,128]{1,0:T(8,128)S(1)}, u32[]{:S(2)}, u32[]{:S(2)}) collective-permute-start(f32[784,128]{1,0:T(8,128)S(1)} %relay.4), channel_id=1, source_target_pairs={{0,6},{1,7},{2,0},{3,1},{4,2},{5,3},{6,4},{7,5},{8,14},{9,15},{10,... | collective-permute-start | bytes 1204232 | tf_op jit(solution)/shard_map/ppermute | solution.py:732
  23.0 1.5 %collective-permute-start.3 = (f32[168,128]{1,0:T(8,128)S(1)}, f32[168,128]{1,0:T(8,128)S(1)}, u32[]{:S(2)}, u32[]{:S(2)}) collective-permute-start(f32[168,128]{1,0:T(8,128)S(1)} %get-tuple-element.29), channel_id=1, source_target_pairs={{0,8},{8,0},{16,24},{24,16},{1,9},{9,1},{17,25},{25,17},{2,10},{10... | collective-permute-start | bytes 258056 | tf_op jit(solution)/shard_map/ppermute | solution.py:57
  24.5 0.9 %collective-permute-start.4 = (f32[168,128]{1,0:T(8,128)S(1)}, f32[168,128]{1,0:T(8,128)S(1)}, u32[]{:S(2)}, u32[]{:S(2)}) collective-permute-start(f32[168,128]{1,0:T(8,128)S(1)} %get-tuple-element.30), channel_id=1, source_target_pairs={{8,16},{16,8},{24,0},{0,24},{9,17},{17,9},{25,1},{1,25},{10,18},{1... | collective-permute-start | bytes 258056 | tf_op jit(solution)/shard_map/ppermute | solution.py:57
  25.4 1.2 %collective-permute-done.3.near = f32[168,128]{1,0:T(8,128)S(1)} collective-permute-done((f32[168,128]{1,0:T(8,128)S(1)}, f32[168,128]{1,0:T(8,128)S(1)}, u32[]{:S(2)}, u32[]{:S(2)}) %collective-permute-start.3) | collective-permute-done | bytes 86048 | tf_op jit(solution)/shard_map/ppermute | solution.py:57
  26.7 3.3 %collective-permute-done.4.across = f32[168,128]{1,0:T(8,128)S(1)} collective-permute-done((f32[168,128]{1,0:T(8,128)S(1)}, f32[168,128]{1,0:T(8,128)S(1)}, u32[]{:S(2)}, u32[]{:S(2)}) %collective-permute-start.4) | collective-permute-done | bytes 86048 | tf_op jit(solution)/shard_map/ppermute | solution.py:57
  29.9 4.3 %combine.1.rest_3_.coef_ref = f32[9128,128]{1,0:T(8,128)S(1)} custom-call(f32[4368,128]{1,0:T(8,128)S(1)} %get-tuple-element.28.ring_ref.rest_1_, f32[168,128]{1,0:T(8,128)S(1)} %collective-permute-done.3.near, f32[168,128]{1,0:T(8,128)S(1)} %collective-permute-done.4.across), custom_call_target="tpu_custom_call" | custom-call | tf_op jit(solution)/shard_map/combine/pallas_call | solution.py:460
  34.2 6.7 %collective-permute-done.7.rest_0_ = f32[784,128]{1,0:T(8,128)S(1)} collective-permute-done((f32[784,128]{1,0:T(8,128)S(1)}, f32[784,128]{1,0:T(8,128)S(1)}, u32[]{:S(2)}, u32[]{:S(2)}) %collective-permute-start.7) | collective-permute-done | bytes 401440 | tf_op jit(solution)/shard_map/ppermute | solution.py:738
  40.9 2.0 %scatter_more.1.rest_2_ = f32[7280,128]{1,0:T(8,128)S(1)} custom-call(s32[1,2560]{1,0:T(1,128)S(1)} %constant_dynamic-update-slice_fusion.table_ref, f32[784,128]{1,0:T(8,128)S(1)} %collective-permute-done.7.rest_0_, f32[7280,128]{1,0:T(8,128)S(1)} %scatter_own.1.after.rest_1_), custom_call_target="tpu_custom_call", output_to_operand_aliasing={{}: (2, {})} | custom-call | tf_op jit(solution)/shard_map/scatter_more/pallas_call | solution.py:347
  42.9 5.5 %collective-permute-done.6.rest_1_ = f32[784,128]{1,0:T(8,128)S(1)} collective-permute-done((f32[784,128]{1,0:T(8,128)S(1)}, f32[784,128]{1,0:T(8,128)S(1)}, u32[]{:S(2)}, u32[]{:S(2)}) %collective-permute-start.6) | collective-permute-done | bytes 401440 | tf_op jit(solution)/shard_map/ppermute | solution.py:732
  48.3 3.1 %scatter_last.1 = (f32[7280,128]{1,0:T(8,128)S(1)}, f32[480,128]{1,0:T(8,128)S(1)}, f32[480,128]{1,0:T(8,128)S(1)}) custom-call(s32[1,2560]{1,0:T(1,128)S(1)} %constant_dynamic-update-slice_fusion.table_ref, f32[784,128]{1,0:T(8,128)S(1)} %collective-permute-done.5.rest_0_, ...), custom_call_target="tpu_custom_call", output_to_operand_aliasing={{0}: (3, {})} | custom-call | tf_op jit(solution)/shard_map/scatter_last/pallas_call | solution.py:347
  51.4 0.6 collective-permute-start.8
  52.0 4.7 %collective-permute-start.9 = (f32[480,128]{1,0:T(8,128)S(1)}, f32[480,128]{1,0:T(8,128)S(1)}, u32[]{:S(2)}, u32[]{:S(2)}) collective-permute-start(f32[480,128]{1,0:T(8,128)S(1)} %get-tuple-element.36), channel_id=1, source_target_pairs={{1,2},{2,1},{3,4},{4,3},{5,6},{6,5},{9,10},{10,9},{11,12},{12,11},... | collective-permute-start | bytes 737288 | tf_op jit(solution)/shard_map/ppermute | solution.py:57
  56.7 4.9 %early.1.mid_in = f32[6520,128]{1,0:T(8,128)S(1)} custom-call(f32[9128,128]{1,0:T(8,128)S(1)} %combine.1.rest_3_.coef_ref, f32[7280,128]{1,0:T(8,128)S(1)} %get-tuple-element.34.state_in.state), custom_call_target="tpu_custom_call" | custom-call | tf_op jit(solution)/shard_map/early/pallas_call | solution.py:579
  61.6 0.0 collective-permute-done.9.across
  61.6 0.4 insert.1
  62.0 1.9 %collective-permute-start.10 = (f32[280,128]{1,0:T(8,128)S(1)}, f32[280,128]{1,0:T(8,128)S(1)}, u32[]{:S(2)}, u32[]{:S(2)}) collective-permute-start(f32[280,128]{1,0:T(8,128)S(1)} %get-tuple-element.39), channel_id=1, source_target_pairs={{0,8},{8,0},{16,24},{24,16},{1,9},{9,1},{17,25},{25,17},{2,10},{10... | collective-permute-start | bytes 430088 | tf_op jit(solution)/shard_map/ppermute | solution.py:57
  63.9 1.2 %collective-permute-start.11 = (f32[280,128]{1,0:T(8,128)S(1)}, f32[280,128]{1,0:T(8,128)S(1)}, u32[]{:S(2)}, u32[]{:S(2)}) collective-permute-start(f32[280,128]{1,0:T(8,128)S(1)} %get-tuple-element.40), channel_id=1, source_target_pairs={{8,16},{16,8},{24,0},{0,24},{9,17},{17,9},{25,1},{1,25},{10,18},{1... | collective-permute-start | bytes 430088 | tf_op jit(solution)/shard_map/ppermute | solution.py:57
  65.1 7.6 %inner.1 = (f32[6520,128]{1,0:T(8,128)S(1)}, f32[5760,128]{1,0:T(8,128)}) custom-call(f32[9128,128]{1,0:T(8,128)S(1)} %combine.1.rest_3_.coef_ref, f32[7280,128]{1,0:T(8,128)S(1)} %get-tuple-element.37.state.state_in, f32[6520,128]{1,0:T(8,128)S(1)} %early.1.mid_in), custom_call_target="tpu_custom_call", output_to_operand_aliasing={{0}: (2, {})} | custom-call | tf_op jit(solution)/shard_map/inner/pallas_call | solution.py:623
  72.8 0.0 collective-permute-done.10.near
  72.8 0.0 collective-permute-done.11.across
  72.8 1.7 %outer.1 = (f32[7280,128]{1,0:T(8,128)S(1)}, f32[6520,128]{1,0:T(8,128)S(1)}, f32[5760,128]{1,0:T(8,128)}) custom-call(f32[9128,128]{1,0:T(8,128)S(1)} %combine.1.rest_3_.coef_ref, f32[7280,128]{1,0:T(8,128)S(1)} %get-tuple-element.37.state.state_in, ...), custom_call_target="tpu_custom_call", output_to_operand_aliasing={{0}: (1, {}), {1}: (2, {}), {2}: (5, {})} | custom-call | tf_op jit(solution)/shard_map/outer/pallas_call | solution.py:683
  (10 shorter events, 0.1 us)
Async XLA Ops:
  4.8 14.1 %collective-permute-start = (f32[288,128]{1,0:T(8,128)S(1)}, f32[288,128]{1,0:T(8,128)S(1)}, u32[]{:S(2)}, u32[]{:S(2)}) collective-permute-start(f32[288,128]{1,0:T(8,128)S(1)} %get-tuple-element.24), channel_id=1, source_target_pairs={{0,1},{1,0},{2,3},{3,2},{4,5},{5,4},{6,7},{7,6},{8,9},{9,8},{10,11... | collective-permute-start | bytes 442376 | tf_op jit(solution)/shard_map/ppermute | solution.py:57
  4.9 14.0 %collective-permute-start.1 = (f32[288,128]{1,0:T(8,128)S(1)}, f32[288,128]{1,0:T(8,128)S(1)}, u32[]{:S(2)}, u32[]{:S(2)}) collective-permute-start(f32[288,128]{1,0:T(8,128)S(1)} %get-tuple-element.25), channel_id=1, source_target_pairs={{1,2},{2,1},{3,4},{4,3},{5,6},{6,5},{9,10},{10,9},{11,12},{12,11},... | collective-permute-start | bytes 442376 | tf_op jit(solution)/shard_map/ppermute | solution.py:57
  9.5 2.4 %collective-permute-start.2 = (f32[1568,128]{1,0:T(8,128)S(1)}, f32[1568,128]{1,0:T(8,128)S(1)}, u32[]{:S(2)}, u32[]{:S(2)}) collective-permute-start(f32[1568,128]{1,0:T(8,128)S(1)} %get-tuple-element.27), channel_id=1, source_target_pairs={{0,1},{1,0},{2,3},{3,2},{4,5},{5,4},{6,7},{7,6},{8,9},{9,8},{10,11... | collective-permute-start | bytes 2408456 | tf_op jit(solution)/shard_map/ppermute | solution.py:721
  11.9 29.0 %collective-permute-start.7 = (f32[784,128]{1,0:T(8,128)S(1)}, f32[784,128]{1,0:T(8,128)S(1)}, u32[]{:S(2)}, u32[]{:S(2)}) collective-permute-start(f32[784,128]{1,0:T(8,128)S(1)} %relay.5), channel_id=1, source_target_pairs={{0,4},{1,5},{2,6},{3,7},{4,0},{5,1},{6,2},{7,3},{8,12},{9,13},{10,... | collective-permute-start | bytes 1204232 | tf_op jit(solution)/shard_map/ppermute | solution.py:738
  17.6 25.2 %collective-permute-start.5 = (f32[784,128]{1,0:T(8,128)S(1)}, f32[784,128]{1,0:T(8,128)S(1)}, u32[]{:S(2)}, u32[]{:S(2)}) collective-permute-start(f32[784,128]{1,0:T(8,128)S(1)} %relay.3), channel_id=1, source_target_pairs={{0,2},{1,3},{2,4},{3,5},{4,6},{5,7},{6,0},{7,1},{8,10},{9,11},{10,... | collective-permute-start | bytes 1204232 | tf_op jit(solution)/shard_map/ppermute | solution.py:732
  20.9 27.5 %collective-permute-start.6 = (f32[784,128]{1,0:T(8,128)S(1)}, f32[784,128]{1,0:T(8,128)S(1)}, u32[]{:S(2)}, u32[]{:S(2)}) collective-permute-start(f32[784,128]{1,0:T(8,128)S(1)} %relay.4), channel_id=1, source_target_pairs={{0,6},{1,7},{2,0},{3,1},{4,2},{5,3},{6,4},{7,5},{8,14},{9,15},{10,... | collective-permute-start | bytes 1204232 | tf_op jit(solution)/shard_map/ppermute | solution.py:732
  23.0 3.7 %collective-permute-start.3 = (f32[168,128]{1,0:T(8,128)S(1)}, f32[168,128]{1,0:T(8,128)S(1)}, u32[]{:S(2)}, u32[]{:S(2)}) collective-permute-start(f32[168,128]{1,0:T(8,128)S(1)} %get-tuple-element.29), channel_id=1, source_target_pairs={{0,8},{8,0},{16,24},{24,16},{1,9},{9,1},{17,25},{25,17},{2,10},{10... | collective-permute-start | bytes 258056 | tf_op jit(solution)/shard_map/ppermute | solution.py:57
  24.5 5.4 %collective-permute-start.4 = (f32[168,128]{1,0:T(8,128)S(1)}, f32[168,128]{1,0:T(8,128)S(1)}, u32[]{:S(2)}, u32[]{:S(2)}) collective-permute-start(f32[168,128]{1,0:T(8,128)S(1)} %get-tuple-element.30), channel_id=1, source_target_pairs={{8,16},{16,8},{24,0},{0,24},{9,17},{17,9},{25,1},{1,25},{10,18},{1... | collective-permute-start | bytes 258056 | tf_op jit(solution)/shard_map/ppermute | solution.py:57
  51.4 10.1 %collective-permute-start.8 = (f32[480,128]{1,0:T(8,128)S(1)}, f32[480,128]{1,0:T(8,128)S(1)}, u32[]{:S(2)}, u32[]{:S(2)}) collective-permute-start(f32[480,128]{1,0:T(8,128)S(1)} %get-tuple-element.35), channel_id=1, source_target_pairs={{0,1},{1,0},{2,3},{3,2},{4,5},{5,4},{6,7},{7,6},{8,9},{9,8},{10,11... | collective-permute-start | bytes 737288 | tf_op jit(solution)/shard_map/ppermute | solution.py:57
  52.0 9.6 %collective-permute-start.9 = (f32[480,128]{1,0:T(8,128)S(1)}, f32[480,128]{1,0:T(8,128)S(1)}, u32[]{:S(2)}, u32[]{:S(2)}) collective-permute-start(f32[480,128]{1,0:T(8,128)S(1)} %get-tuple-element.36), channel_id=1, source_target_pairs={{1,2},{2,1},{3,4},{4,3},{5,6},{6,5},{9,10},{10,9},{11,12},{12,11},... | collective-permute-start | bytes 737288 | tf_op jit(solution)/shard_map/ppermute | solution.py:57
  62.0 10.8 %collective-permute-start.10 = (f32[280,128]{1,0:T(8,128)S(1)}, f32[280,128]{1,0:T(8,128)S(1)}, u32[]{:S(2)}, u32[]{:S(2)}) collective-permute-start(f32[280,128]{1,0:T(8,128)S(1)} %get-tuple-element.39), channel_id=1, source_target_pairs={{0,8},{8,0},{16,24},{24,16},{1,9},{9,1},{17,25},{25,17},{2,10},{10... | collective-permute-start | bytes 430088 | tf_op jit(solution)/shard_map/ppermute | solution.py:57
  63.9 8.9 %collective-permute-start.11 = (f32[280,128]{1,0:T(8,128)S(1)}, f32[280,128]{1,0:T(8,128)S(1)}, u32[]{:S(2)}, u32[]{:S(2)}) collective-permute-start(f32[280,128]{1,0:T(8,128)S(1)} %get-tuple-element.40), channel_id=1, source_target_pairs={{8,16},{16,8},{24,0},{0,24},{9,17},{17,9},{25,1},{1,25},{10,18},{1... | collective-permute-start | bytes 430088 | tf_op jit(solution)/shard_map/ppermute | solution.py:57
